TPU v7x, 256 devices: a whole 4x4x8 slice. The times are simulated.
256 devices in a mesh: ia: 4 (over y), ja: 16 (over z, core), ka: 4 (over x).
Axes of the slice: x: 4, y: 4, z: 8, core: 2. Of those that a mesh axis runs over, the one named last changes fastest.
Arguments:
- tensor: bfloat16 [64, 4096, 4096], P('ia', 'ja', 'ka'), may hold values from -6 to 6
- factor_j: bfloat16 [25, 4096], P(None, ('ja', 'ka', 'ia'))
- factor_k: bfloat16 [25, 4096], P(None, ('ka', 'ja'))
Outputs:
- y_part: float32 [25, 64, 4096], P(None, 'ia', ('ja', 'ka'))
- new_factor: float32 [25, 64], P(None, 'ia')
All inputs are finite; a program needn't handle non-finite values.
Results may differ from a plain program's by a relative error of at most 0.0003.
Values may be sent and summed in bfloat16 or wider, within the bound.
No kernel may reach another device: no remote copies, remote signals or barrier semaphores. Data moves between devices by JAX's collectives and lax.ppermute only.
A program may use at most 64 MiB of HBM per device.

v0:
```python
import functools

import jax
import jax.numpy as jnp
from jax import lax
from jax.experimental import pallas as pl
from jax.experimental.pallas import tpu as pltpu
from jax.sharding import PartitionSpec as P

f32, bf16 = jnp.float32, jnp.bfloat16
R = 25
VM = pl.BlockSpec(memory_space=pltpu.VMEM)
HB = pl.BlockSpec(memory_space=pltpu.HBM)
TILES, BODY, MSG = 8, 200, 208
DIAGONALS = 13
BLOCK = 13


def lanes_of(shape):
    return lax.broadcasted_iota(jnp.int32, shape, 1)


def sublanes_of(shape):
    return lax.broadcasted_iota(jnp.int32, shape, 0)


def pad_rows(x, rows):
    return jnp.concatenate([x, jnp.zeros((rows - x.shape[0], x.shape[1]), x.dtype)], axis=0)


def fold(g):
    return jnp.concatenate([g[8 * q : 8 * q + 8] for q in range(4)], axis=1)


def unfold(g):
    return jnp.concatenate([g[:, 32 * q : 32 * q + 32] for q in range(4)], axis=0)


def transposed(x):
    rows = -(-x.shape[1] // 8) * 8
    x = jnp.concatenate([x, jnp.zeros((x.shape[0], 128 - x.shape[1]), x.dtype)], axis=1)
    return pad_rows(x, 128).T[0:rows, 0 : x.shape[0]]


def pack_kernel(k_ref, out_ref, k_vmem, sem):
    copy = pltpu.make_async_copy(k_ref, k_vmem, sem)
    copy.start()
    copy.wait()
    k = pad_rows(k_vmem[...].astype(f32), 32)
    folded = jnp.concatenate([k[0:16], k[16:32]], axis=1).astype(bf16)
    out_ref[...] = jnp.broadcast_to(folded[None], out_ref.shape)


def factor_kernel(j0, j1, j2, j3, out_ref):
    rows = jnp.concatenate([j[...].astype(f32) for j in (j0, j3, j2, j1)], axis=0)
    b = transposed(rows)
    out_ref[0:32, :] = pltpu.roll(jnp.concatenate([b, b], axis=1), lax.axis_index("ia") * 16, 1)
    rows = jnp.concatenate([rows, rows, jnp.zeros((64, 128 - 2 * R), f32)], axis=1)
    turned = [pltpu.roll(rows, 128 - d, 1) if d else rows for d in range(DIAGONALS)]
    diagonals = [jnp.sum(rows * x, axis=0, keepdims=True) for x in turned]
    diagonals = pad_rows(jnp.concatenate(diagonals, axis=0), 16)
    low = lanes_of((8, 128)) < 32
    out_ref[32:40, :] = jnp.where(low, diagonals[0:8], pltpu.roll(diagonals[8:16], 32, 1))


def part_copy(t_ref, dst, s, sem):
    dest = lax.rem(lax.axis_index("ka") + s, 4)
    block = t_ref.at[:, pl.ds(pl.multiple_of(dest * 64, 64), 64), :]
    return pltpu.make_async_copy(block, dst, sem)


def load_kernel(t_ref, out_ref, sem):
    copy = part_copy(t_ref, out_ref, 2, sem)
    copy.start()
    copy.wait()


def contract_kernel(c_ref, part_ref, t_ref, *refs):
    msgs, held_ref, sems = refs[0:4], refs[4], refs[5]
    copies = {s: part_copy(t_ref, held_ref.at[n], s, sems.at[n]) for n, s in enumerate((1, 3, 0))}
    for copy in copies.values():
        copy.start()
    blocks = [c_ref[p].astype(f32) for p in range(16)]
    low = lanes_of((16, 128)) < 64
    tops, bottoms = [], []
    for a, b in zip(blocks[0::2], blocks[1::2]):
        tops.append(jnp.where(low, a, pltpu.roll(b, 64, 1)))
        bottoms.append(jnp.where(low, pltpu.roll(a, 64, 1), b))
    c = jnp.concatenate([jnp.concatenate(tops, axis=1), jnp.concatenate(bottoms, axis=1)], axis=0).astype(bf16)
    nt = (((1,), (1,)), ((), ()))
    gram = fold(lax.dot_general(c, c, nt, preferred_element_type=f32))
    for s in (2, 1, 3, 0):
        if s in copies:
            copies[s].wait()
        block = held_ref[(1, 3, 0).index(s)] if s in copies else part_ref[...]
        y = lax.dot_general(c, block.reshape(1024, 1024), nt, preferred_element_type=f32)
        for t in range(TILES):
            msgs[s][24 * t : 24 * t + 24, :] = y[0:24, 128 * t : 128 * t + 128]
            msgs[s][192 + t : 193 + t, :] = y[24:25, 128 * t : 128 * t + 128]
        msgs[s][BODY:MSG, :] = gram


def partial_kernel(y0, y1, y2, y3, b0, b1, b2, b3, pay_ref):
    ys, bs = (y0, y1, y2, y3), (b0, b1, b2, b3)
    lane24, low24 = lanes_of((24, 128)), lanes_of((24, 128)) < 64
    m = jnp.zeros((24, 128), f32)
    for t in range(TILES):
        at = slice(24 * t, 24 * t + 24)
        p = functools.reduce(jnp.add, [y[at, :] * b[0:24, :] for y, b in zip(ys, bs)])
        m = jnp.where(lane24 == 2 * t, jnp.sum(jnp.where(low24, p, 0.0), axis=1, keepdims=True), m)
        m = jnp.where(lane24 == 2 * t + 1, jnp.sum(jnp.where(low24, 0.0, p), axis=1, keepdims=True), m)
    p = functools.reduce(jnp.add, [y[192:200, :] * b[24:25, :] for y, b in zip(ys, bs)])
    low8 = lanes_of((8, 128)) < 64
    last = [jnp.sum(jnp.where(keep, p, 0.0), axis=1, keepdims=True) for keep in (low8, ~low8)]
    d = (b0[32:40, :] + b1[32:40, :]) + (b2[32:40, :] + b3[32:40, :])
    d = jnp.concatenate([d[:, 0:32], d[:, 32:64]], axis=0)
    d = pltpu.roll(d, lax.rem(16 - 4 * lax.axis_index("ka"), 16), 0)[0:4, 0:R]
    pay = [m[4 * q : 4 * q + 4, 0:16] for q in range(6)] + [d]
    pay += [x[v : v + 4] for v in (0, 4) for x in last] + [jnp.zeros((4, 3), f32)]
    pay_ref[...] = jnp.broadcast_to(jnp.concatenate(pay, axis=1)[None], pay_ref.shape)


def sum_kernel(y0, y1, y2, y3, y_ref, gk_ref):
    def total(at):
        return (y0[at, :] + y1[at, :]) + (y2[at, :] + y3[at, :])

    for t in range(TILES):
        s = total(slice(24 * t, 24 * t + 24))
        y_ref[pl.ds(2 * t, 24, stride=16), :] = s[:, 0:64]
        y_ref[pl.ds(2 * t + 1, 24, stride=16), :] = s[:, 64:128]
    s = total(slice(192, 200))
    y_ref[pl.ds(384, 8, stride=2), :] = s[:, 0:64]
    y_ref[pl.ds(385, 8, stride=2), :] = s[:, 64:128]
    gk_ref[...] = total(slice(BODY, MSG))


def solve_kernel(x_ref, gk_ref, out_ref):
    x = jnp.sum(x_ref[...].reshape(16, 4, 4, 128), axis=0)
    d = jnp.concatenate([x[q][:, 96 : 96 + R] for q in range(4)], axis=0)
    x = (x[0] + x[1]) + (x[2] + x[3])
    lane, sub = lanes_of((4, 16)), sublanes_of((4, 16))
    last = jnp.zeros((4, 16), f32)
    for q in range(4):
        here = (lane // 8 == q // 2) & (lane % 2 == q % 2) & (lane // 2 % 4 == sub)
        last = jnp.where(here, x[:, 121 + q : 122 + q], last)
    last = jnp.sum(last, axis=0, keepdims=True)
    m = pad_rows(jnp.concatenate([x[:, 16 * q : 16 * q + 16] for q in range(6)] + [last], axis=0), 32)
    row, lane = sublanes_of((32, 32)), lanes_of((32, 32))
    d = jnp.concatenate([d, jnp.zeros((16, 32 - R), f32)], axis=1)
    apart = jnp.where(row < lane, row - lane + R, row - lane)
    gram = jnp.zeros((32, 32), f32)
    for q in range(1, DIAGONALS):
        gram = jnp.where(apart == q, d[q : q + 1, :], gram)
    gram = gram + transposed(gram)
    gram = jnp.where(apart == 0, d[0:1, :], gram)
    n = jnp.where((row < R) & (lane < R), gram * unfold(gk_ref[...]), 0.0)
    a = jnp.concatenate([n, m, jnp.zeros((32, 80), f32)], axis=1)
    row_at = sublanes_of((32, 128))
    for first in range(0, R, BLOCK):
        cols = [jnp.broadcast_to(a[:, p : p + 1], (32, 128)) for p in range(first, min(first + BLOCK, R))]
        for q in range(len(cols)):
            p = first + q
            scale = 1.0 / cols[q][p : p + 1, :]

            def eliminate(x):
                row = jnp.broadcast_to(x[p : p + 1, :] * scale, (32, 128))
                return jnp.where(row_at == p, row, x - cols[q] * row)

            a = eliminate(a)
            cols[q + 1 :] = [eliminate(x) for x in cols[q + 1 :]]
    out_ref[...] = pad_rows(a, 128).T[32:48, 0:R]


def call(kernel, out, specs, flops=0, nbytes=0, scratch=()):
    return pl.pallas_call(
        kernel,
        out_shape=out,
        in_specs=specs,
        out_specs=jax.tree.map(lambda _: VM, out),
        scratch_shapes=scratch,
        compiler_params=pltpu.CompilerParams(vmem_limit_bytes=10 * 2**20),
        cost_estimate=pl.CostEstimate(flops=flops, bytes_accessed=nbytes, transcendentals=0),
    )


def shift(x, axis, by, n):
    return lax.ppermute(x, axis, [(i, (i + by) % n) for i in range(n)])


def per_device(tensor, factor_j, factor_k):
    sds = jax.ShapeDtypeStruct
    dma = pltpu.SemaphoreType.DMA
    factor_k = pltpu.with_memory_space_constraint(factor_k, pltpu.HBM)
    tensor = pltpu.with_memory_space_constraint(tensor, pltpu.HBM)
    j0 = factor_j.T
    js = [shift(j0, "ia", s, 4) for s in (1, 2, 3)]
    packed = call(pack_kernel, sds((16, 16, 128), bf16), [HB], scratch=[pltpu.VMEM((R, 64), bf16), dma(())])(factor_k)
    c = lax.all_to_all(packed, ("z", "c"), 0, 0, tiled=True)
    part = call(load_kernel, sds((16, 64, 1024), bf16), [HB], 0, 2**22, [dma(())])(tensor)
    part = pltpu.with_memory_space_constraint(part, pltpu.VMEM)
    b = call(factor_kernel, sds((40, 128), f32), [VM] * 4, 2**33, 2**20)(j0, *js)
    bs = [b] + [shift(b, "ka", 4 - s, 4) for s in (1, 2, 3)]
    msgs = call(
        contract_kernel, [sds((MSG, 128), f32)] * 4, [VM, VM, HB], 2**34, 2**23,
        [pltpu.VMEM((3, 16, 64, 1024), bf16), dma((3,))],
    )(c, part, tensor)
    got = [shift(msgs[s], "ka", s, 4) for s in (1, 2, 3)]
    pay = call(partial_kernel, sds((64, 4, 128), f32), [VM] * 8)(*msgs, *bs)
    pay = lax.all_to_all(pay, ("z", "c", "ka"), 0, 0, tiled=True)
    y, gram_k = call(sum_kernel, [sds((400, 64), f32), sds((8, 128), f32)], [VM] * 4, 0, 2**21)(msgs[0], *got)
    new_factor = call(solve_kernel, sds((16, R), f32), [VM] * 2)(pay, gram_k)
    return y.reshape(R, 16, 64), new_factor.T


def solution(mesh):
    ia, ja, ka = (mesh.shape[a] for a in ("ia", "ja", "ka"))
    mesh = jax.sharding.Mesh(mesh.devices.reshape(ia, ja // 2, 2, ka), ("ia", "z", "c", "ka"))
    in_specs = (P("ia", ("z", "c"), "ka"), P(None, ("z", "c", "ka", "ia")), P(None, ("ka", "z", "c")))
    out_specs = (P(None, "ia", ("z", "c", "ka")), P(None, "ia"))
    return jax.shard_map(
        per_device, mesh=mesh, in_specs=in_specs, out_specs=out_specs, check_vma=False
    )
```

profile of v0, /device:TPU:1, one launch (start us, length us, event | category | flops | bytes accessed | tf_op | source)
XLA Modules:
  0.0 51.7 jit_solution(5157805595837778254)
XLA Ops:
  0.6 0.0 copy-start
  0.6 2.2 %collective-permute-start.3 = (bf16[16,25]{1,0:T(8,128)(2,1)}, bf16[16,25]{1,0:T(8,128)(2,1)S(1)}, u32[]{:S(2)}, u32[]{:S(2)}) collective-permute-start(bf16[16,25]{1,0:T(8,128)(2,1)} %bitcast.3), channel_id=1, source_target_pairs={{0,64},{64,128},{128,192},{192,0},{1,65},{65,129},{129,193},{193,1... | collective-permute-start | bytes 2408 | tf_op jit(solution)/shard_map/ppermute | solution.py:187
  2.8 2.6 %collective-permute-start.4 = (bf16[16,25]{1,0:T(8,128)(2,1)}, bf16[16,25]{1,0:T(8,128)(2,1)S(1)}, u32[]{:S(2)}, u32[]{:S(2)}) collective-permute-start(bf16[16,25]{1,0:T(8,128)(2,1)} %bitcast.4), channel_id=1, source_target_pairs={{0,128},{64,192},{128,0},{192,64},{1,129},{65,193},{129,1},{193,65... | collective-permute-start | bytes 2408 | tf_op jit(solution)/shard_map/ppermute | solution.py:187
  5.5 1.1 %collective-permute-start.5 = (bf16[16,25]{1,0:T(8,128)(2,1)}, bf16[16,25]{1,0:T(8,128)(2,1)S(1)}, u32[]{:S(2)}, u32[]{:S(2)}) collective-permute-start(bf16[16,25]{1,0:T(8,128)(2,1)} %bitcast.5), channel_id=1, source_target_pairs={{0,192},{64,0},{128,64},{192,128},{1,193},{65,1},{129,65},{193,129... | collective-permute-start | bytes 2408 | tf_op jit(solution)/shard_map/ppermute | solution.py:187
  6.5 1.4 %shard_map.50 = bf16[16,16,128]{2,1,0:T(8,128)(2,1)} custom-call(bf16[25,64]{1,0:T(8,128)(2,1)} %k_ref.1), custom_call_target="tpu_custom_call" | custom-call | tf_op jit(solution)/shard_map/pallas_call | solution.py:197
  8.0 10.0 %all-to-all-start = ((bf16[16,16,128]{2,1,0:T(8,128)(2,1)}), bf16[16,16,128]{2,1,0:T(8,128)(2,1)S(1)}, u32[]{:S(2)}, u32[]{:S(2)}) async-start(bf16[16,16,128]{2,1,0:T(8,128)(2,1)} %shard_map.50), calls=%async_computation | async-start | bytes 131072 | tf_op jit(solution)/shard_map/all_to_all | solution.py:198
  18.0 1.6 %shard_map.51.part_ref = bf16[16,64,1024]{2,1,0:T(8,128)(2,1)S(1)} custom-call(bf16[16,256,1024]{2,1,0:T(8,128)(2,1)} %t_ref.3), custom_call_target="tpu_custom_call" | custom-call | bytes 4194304 | tf_op jit(solution)/shard_map/pallas_call | solution.py:199
  19.6 0.0 collective-permute-done.3.j1
  19.6 0.0 collective-permute-done.4.j2
  19.6 0.0 collective-permute-done.5.j3
  19.6 0.0 copy-done
  19.6 0.3 shard_map.54.b0
  19.9 2.5 %collective-permute-start.6 = (f32[40,128]{1,0:T(8,128)S(1)}, f32[40,128]{1,0:T(8,128)S(1)}, u32[]{:S(2)}, u32[]{:S(2)}) collective-permute-start(f32[40,128]{1,0:T(8,128)S(1)} %shard_map.54.b0), channel_id=1, source_target_pairs={{0,3},{1,0},{2,1},{3,2},{4,7},{5,4},{6,5},{7,6},{8,11},{9,8},{10,9... | collective-permute-start | bytes 61448 | tf_op jit(solution)/shard_map/ppermute | solution.py:187
  22.4 0.5 %collective-permute-start.7 = (f32[40,128]{1,0:T(8,128)S(1)}, f32[40,128]{1,0:T(8,128)S(1)}, u32[]{:S(2)}, u32[]{:S(2)}) collective-permute-start(f32[40,128]{1,0:T(8,128)S(1)} %shard_map.54.b0), channel_id=1, source_target_pairs={{0,2},{1,3},{2,0},{3,1},{4,6},{5,7},{6,4},{7,5},{8,10},{9,11},{10,... | collective-permute-start | bytes 61448 | tf_op jit(solution)/shard_map/ppermute | solution.py:187
  22.9 0.6 %collective-permute-start.8 = (f32[40,128]{1,0:T(8,128)S(1)}, f32[40,128]{1,0:T(8,128)S(1)}, u32[]{:S(2)}, u32[]{:S(2)}) collective-permute-start(f32[40,128]{1,0:T(8,128)S(1)} %shard_map.54.b0), channel_id=1, source_target_pairs={{0,1},{1,2},{2,3},{3,0},{4,5},{5,6},{6,7},{7,4},{8,9},{9,10},{10,1... | collective-permute-start | bytes 61448 | tf_op jit(solution)/shard_map/ppermute | solution.py:187
  23.5 2.2 %all-to-all-done.c_ref = bf16[16,16,128]{2,1,0:T(8,128)(2,1)S(1)} async-done(((bf16[16,16,128]{2,1,0:T(8,128)(2,1)}), bf16[16,16,128]{2,1,0:T(8,128)(2,1)S(1)}, u32[]{:S(2)}, u32[]{:S(2)}) %all-to-all-start) | async-done | bytes 65568 | tf_op jit(solution)/shard_map/all_to_all | solution.py:198
  25.8 4.5 %shard_map.52 = (f32[208,128]{1,0:T(8,128)S(1)}, f32[208,128]{1,0:T(8,128)S(1)}, f32[208,128]{1,0:T(8,128)S(1)}, f32[208,128]{1,0:T(8,128)S(1)}) custom-call(bf16[16,16,128]{2,1,0:T(8,128)(2,1)S(1)} %all-to-all-done.c_ref, bf16[16,64,1024]{2,1,0:T(8,128)(2,1)S(1)} %shard_map.51.part_ref, bf16[16,256,1024]{2,1,0:T(8,128)(2,1)} %t_ref.3), custom_call_target="tpu_custom_call" | custom-call | flops 17179869184 | bytes 8388608 | tf_op jit(solution)/shard_map/pallas_call | solution.py:203
  30.2 0.0 collective-permute-done.6.b1
  30.2 0.0 collective-permute-done.7.b2
  30.3 0.0 collective-permute-done.8.b3
  30.3 0.9 %shard_map.55 = f32[64,4,128]{2,1,0:T(4,128)} custom-call(f32[208,128]{1,0:T(8,128)S(1)} %get-tuple-element.8.y0, f32[208,128]{1,0:T(8,128)S(1)} %get-tuple-element.9.y1, f32[208,128]{1,0:T(8,128)S(1)} %get-tuple-element.10.y2, f32[208,128]{1,0:T(8,128)S(1)} %get-tuple-element.11.y3, f32[40,128]{1,0:T(8,128)S(1)} %shard_map.54.b0, ...), custom_call_target="tpu_custom_call" | custom-call | tf_op jit(solution)/shard_map/pallas_call | solution.py:208
  31.2 8.1 %all-to-all-start.1 = ((f32[64,4,128]{2,1,0:T(4,128)}), f32[64,4,128]{2,1,0:T(4,128)S(1)}, u32[]{:S(2)}, u32[]{:S(2)}) async-start(f32[64,4,128]{2,1,0:T(4,128)} %shard_map.55), calls=%async_computation.1 | async-start | bytes 262144 | tf_op jit(solution)/shard_map/all_to_all | solution.py:209
  39.3 1.5 %collective-permute-start = (f32[208,128]{1,0:T(8,128)S(1)}, f32[208,128]{1,0:T(8,128)S(1)}, u32[]{:S(2)}, u32[]{:S(2)}) collective-permute-start(f32[208,128]{1,0:T(8,128)S(1)} %get-tuple-element.9.y1), channel_id=1, source_target_pairs={{0,1},{1,2},{2,3},{3,0},{4,5},{5,6},{6,7},{7,4},{8,9},{9,10},{10,1... | collective-permute-start | bytes 319496 | tf_op jit(solution)/shard_map/ppermute | solution.py:187
  40.8 2.4 %collective-permute-start.1 = (f32[208,128]{1,0:T(8,128)S(1)}, f32[208,128]{1,0:T(8,128)S(1)}, u32[]{:S(2)}, u32[]{:S(2)}) collective-permute-start(f32[208,128]{1,0:T(8,128)S(1)} %get-tuple-element.10.y2), channel_id=1, source_target_pairs={{0,2},{1,3},{2,0},{3,1},{4,6},{5,7},{6,4},{7,5},{8,10},{9,11},{10,... | collective-permute-start | bytes 319496 | tf_op jit(solution)/shard_map/ppermute | solution.py:187
  43.2 1.2 %collective-permute-start.2 = (f32[208,128]{1,0:T(8,128)S(1)}, f32[208,128]{1,0:T(8,128)S(1)}, u32[]{:S(2)}, u32[]{:S(2)}) collective-permute-start(f32[208,128]{1,0:T(8,128)S(1)} %get-tuple-element.11.y3), channel_id=1, source_target_pairs={{0,3},{1,0},{2,1},{3,2},{4,7},{5,4},{6,5},{7,6},{8,11},{9,8},{10,9... | collective-permute-start | bytes 319496 | tf_op jit(solution)/shard_map/ppermute | solution.py:187
  44.4 0.8 %collective-permute-done.y1 = f32[208,128]{1,0:T(8,128)S(1)} collective-permute-done((f32[208,128]{1,0:T(8,128)S(1)}, f32[208,128]{1,0:T(8,128)S(1)}, u32[]{:S(2)}, u32[]{:S(2)}) %collective-permute-start) | collective-permute-done | bytes 106528 | tf_op jit(solution)/shard_map/ppermute | solution.py:187
  45.2 4.3 %collective-permute-done.1.y2 = f32[208,128]{1,0:T(8,128)S(1)} collective-permute-done((f32[208,128]{1,0:T(8,128)S(1)}, f32[208,128]{1,0:T(8,128)S(1)}, u32[]{:S(2)}, u32[]{:S(2)}) %collective-permute-start.1) | collective-permute-done | bytes 106528 | tf_op jit(solution)/shard_map/ppermute | solution.py:187
  49.5 0.0 collective-permute-done.2.y3
  49.5 0.8 %shard_map.53 = (f32[400,64]{1,0:T(8,128)}, f32[8,128]{1,0:T(8,128)S(1)}) custom-call(f32[208,128]{1,0:T(8,128)S(1)} %get-tuple-element.8.y0, f32[208,128]{1,0:T(8,128)S(1)} %collective-permute-done.y1, f32[208,128]{1,0:T(8,128)S(1)} %collective-permute-done.1.y2, f32[208,128]{1,0:T(8,128)S(1)} %collective-permute-done.2.y3), custom_call_target="tpu_custom_call" | custom-call | bytes 2097152 | tf_op jit(solution)/shard_map/pallas_call | solution.py:210
  50.3 0.0 all-to-all-done.1.x_ref
  50.3 1.4 %shard_map.56 = f32[16,25]{1,0:T(8,128)} custom-call(f32[64,4,128]{2,1,0:T(4,128)S(1)} %all-to-all-done.1.x_ref, f32[8,128]{1,0:T(8,128)S(1)} %get-tuple-element.13.gk_ref), custom_call_target="tpu_custom_call" | custom-call | tf_op jit(solution)/shard_map/pallas_call | solution.py:211
Async XLA Ops:
  0.6 19.0 %copy-start = (bf16[25,16]{0,1:T(8,128)(2,1)S(1)}, bf16[25,16]{0,1:T(8,128)(2,1)}, u32[]{:S(2)}) copy-start(bf16[25,16]{0,1:T(8,128)(2,1)} %param.4) | copy-start | bytes 2404
  0.6 18.9 %collective-permute-start.3 = (bf16[16,25]{1,0:T(8,128)(2,1)}, bf16[16,25]{1,0:T(8,128)(2,1)S(1)}, u32[]{:S(2)}, u32[]{:S(2)}) collective-permute-start(bf16[16,25]{1,0:T(8,128)(2,1)} %bitcast.3), channel_id=1, source_target_pairs={{0,64},{64,128},{128,192},{192,0},{1,65},{65,129},{129,193},{193,1... | collective-permute-start | bytes 2408 | tf_op jit(solution)/shard_map/ppermute | solution.py:187
  2.8 16.7 %collective-permute-start.4 = (bf16[16,25]{1,0:T(8,128)(2,1)}, bf16[16,25]{1,0:T(8,128)(2,1)S(1)}, u32[]{:S(2)}, u32[]{:S(2)}) collective-permute-start(bf16[16,25]{1,0:T(8,128)(2,1)} %bitcast.4), channel_id=1, source_target_pairs={{0,128},{64,192},{128,0},{192,64},{1,129},{65,193},{129,1},{193,65... | collective-permute-start | bytes 2408 | tf_op jit(solution)/shard_map/ppermute | solution.py:187
  5.5 14.1 %collective-permute-start.5 = (bf16[16,25]{1,0:T(8,128)(2,1)}, bf16[16,25]{1,0:T(8,128)(2,1)S(1)}, u32[]{:S(2)}, u32[]{:S(2)}) collective-permute-start(bf16[16,25]{1,0:T(8,128)(2,1)} %bitcast.5), channel_id=1, source_target_pairs={{0,192},{64,0},{128,64},{192,128},{1,193},{65,1},{129,65},{193,129... | collective-permute-start | bytes 2408 | tf_op jit(solution)/shard_map/ppermute | solution.py:187
  8.0 17.8 %all-to-all-start = ((bf16[16,16,128]{2,1,0:T(8,128)(2,1)}), bf16[16,16,128]{2,1,0:T(8,128)(2,1)S(1)}, u32[]{:S(2)}, u32[]{:S(2)}) async-start(bf16[16,16,128]{2,1,0:T(8,128)(2,1)} %shard_map.50), calls=%async_computation | async-start | bytes 131072 | tf_op jit(solution)/shard_map/all_to_all | solution.py:198
  19.9 10.4 %collective-permute-start.6 = (f32[40,128]{1,0:T(8,128)S(1)}, f32[40,128]{1,0:T(8,128)S(1)}, u32[]{:S(2)}, u32[]{:S(2)}) collective-permute-start(f32[40,128]{1,0:T(8,128)S(1)} %shard_map.54.b0), channel_id=1, source_target_pairs={{0,3},{1,0},{2,1},{3,2},{4,7},{5,4},{6,5},{7,6},{8,11},{9,8},{10,9... | collective-permute-start | bytes 61448 | tf_op jit(solution)/shard_map/ppermute | solution.py:187
  22.4 7.8 %collective-permute-start.7 = (f32[40,128]{1,0:T(8,128)S(1)}, f32[40,128]{1,0:T(8,128)S(1)}, u32[]{:S(2)}, u32[]{:S(2)}) collective-permute-start(f32[40,128]{1,0:T(8,128)S(1)} %shard_map.54.b0), channel_id=1, source_target_pairs={{0,2},{1,3},{2,0},{3,1},{4,6},{5,7},{6,4},{7,5},{8,10},{9,11},{10,... | collective-permute-start | bytes 61448 | tf_op jit(solution)/shard_map/ppermute | solution.py:187
  22.9 7.3 %collective-permute-start.8 = (f32[40,128]{1,0:T(8,128)S(1)}, f32[40,128]{1,0:T(8,128)S(1)}, u32[]{:S(2)}, u32[]{:S(2)}) collective-permute-start(f32[40,128]{1,0:T(8,128)S(1)} %shard_map.54.b0), channel_id=1, source_target_pairs={{0,1},{1,2},{2,3},{3,0},{4,5},{5,6},{6,7},{7,4},{8,9},{9,10},{10,1... | collective-permute-start | bytes 61448 | tf_op jit(solution)/shard_map/ppermute | solution.py:187
  31.2 19.2 %all-to-all-start.1 = ((f32[64,4,128]{2,1,0:T(4,128)}), f32[64,4,128]{2,1,0:T(4,128)S(1)}, u32[]{:S(2)}, u32[]{:S(2)}) async-start(f32[64,4,128]{2,1,0:T(4,128)} %shard_map.55), calls=%async_computation.1 | async-start | bytes 262144 | tf_op jit(solution)/shard_map/all_to_all | solution.py:209
  39.3 5.9 %collective-permute-start = (f32[208,128]{1,0:T(8,128)S(1)}, f32[208,128]{1,0:T(8,128)S(1)}, u32[]{:S(2)}, u32[]{:S(2)}) collective-permute-start(f32[208,128]{1,0:T(8,128)S(1)} %get-tuple-element.9.y1), channel_id=1, source_target_pairs={{0,1},{1,2},{2,3},{3,0},{4,5},{5,6},{6,7},{7,4},{8,9},{9,10},{10,1... | collective-permute-start | bytes 319496 | tf_op jit(solution)/shard_map/ppermute | solution.py:187
  40.8 8.7 %collective-permute-start.1 = (f32[208,128]{1,0:T(8,128)S(1)}, f32[208,128]{1,0:T(8,128)S(1)}, u32[]{:S(2)}, u32[]{:S(2)}) collective-permute-start(f32[208,128]{1,0:T(8,128)S(1)} %get-tuple-element.10.y2), channel_id=1, source_target_pairs={{0,2},{1,3},{2,0},{3,1},{4,6},{5,7},{6,4},{7,5},{8,10},{9,11},{10,... | collective-permute-start | bytes 319496 | tf_op jit(solution)/shard_map/ppermute | solution.py:187
  43.2 6.3 %collective-permute-start.2 = (f32[208,128]{1,0:T(8,128)S(1)}, f32[208,128]{1,0:T(8,128)S(1)}, u32[]{:S(2)}, u32[]{:S(2)}) collective-permute-start(f32[208,128]{1,0:T(8,128)S(1)} %get-tuple-element.11.y3), channel_id=1, source_target_pairs={{0,3},{1,0},{2,1},{3,2},{4,7},{5,4},{6,5},{7,6},{8,11},{9,8},{10,9... | collective-permute-start | bytes 319496 | tf_op jit(solution)/shard_map/ppermute | solution.py:187
where the time goes:
time: 52 us; the launch traced here: 51.7 us
  starting transfers between devices  32.8 us (63%)
  Pallas kernels  10.8 us (21%)
  waiting for transfers between devices  7.4 us (14%)
  between operations  0.73 us (1%)
    ppermute x9, starting transfers between devices, shift(): return lax.ppermute(x, axis, [(i, (i + by) % n) for i in range(n)])  14.6 us
    all_to_all x1, starting transfers between devices, per_device(): c = lax.all_to_all(packed, ('z', 'c'), 0, 0, tiled=True)  10 us
    all_to_all x1, starting transfers between devices, per_device(): pay = lax.all_to_all(pay, ('z', 'c', 'ka'), 0, 0, tiled=True)  8.15 us
    ppermute x9, waiting for transfers between devices, shift(): return lax.ppermute(x, axis, [(i, (i + by) % n) for i in range(n)])  5.18 us
    pallas_call x1, Pallas kernels, per_device(): call(contract_kernel, [sds((MSG, 128), f32)] * 4, [VM, VM, HB], 2 ** 34,...  4.46 us
    all_to_all x1, waiting for transfers between devices, per_device(): c = lax.all_to_all(packed, ('z', 'c'), 0, 0, tiled=True)  2.22 us
    pallas_call x1, Pallas kernels, per_device(): call(load_kernel, sds((16, 64, 1024), bf16), [HB], 0, 2 ** 22, [dma(())])  1.6 us
    pallas_call x1, Pallas kernels, per_device(): call(pack_kernel, sds((16, 16, 128), bf16), [HB], scratch=[pltpu.VMEM((R,...  1.41 us
  transfers between devices with their start and end apart: 11, of which 3 were waited for; matrix products, arithmetic and copies ran while one was open for 0% of the time, Pallas kernels for 17%

commit v1 on v0

--- a/solution.py
+++ b/solution.py
@@ -69,17 +69,14 @@
     return pltpu.make_async_copy(block, dst, sem)
 
 
-def load_kernel(t_ref, out_ref, sem):
-    copy = part_copy(t_ref, out_ref, 2, sem)
-    copy.start()
-    copy.wait()
-
-
-def contract_kernel(c_ref, part_ref, t_ref, *refs):
+ORDER = (2, 1, 3, 0)
+
+
+def contract_kernel(c_ref, t_ref, *refs):
     msgs, held_ref, sems = refs[0:4], refs[4], refs[5]
-    copies = {s: part_copy(t_ref, held_ref.at[n], s, sems.at[n]) for n, s in enumerate((1, 3, 0))}
-    for copy in copies.values():
-        copy.start()
+    copies = [part_copy(t_ref, held_ref.at[s], s, sems.at[s]) for s in range(4)]
+    for s in ORDER:
+        copies[s].start()
     blocks = [c_ref[p].astype(f32) for p in range(16)]
     low = lanes_of((16, 128)) < 64
     tops, bottoms = [], []
@@ -89,11 +86,9 @@
     c = jnp.concatenate([jnp.concatenate(tops, axis=1), jnp.concatenate(bottoms, axis=1)], axis=0).astype(bf16)
     nt = (((1,), (1,)), ((), ()))
     gram = fold(lax.dot_general(c, c, nt, preferred_element_type=f32))
-    for s in (2, 1, 3, 0):
-        if s in copies:
-            copies[s].wait()
-        block = held_ref[(1, 3, 0).index(s)] if s in copies else part_ref[...]
-        y = lax.dot_general(c, block.reshape(1024, 1024), nt, preferred_element_type=f32)
+    for s in ORDER:
+        copies[s].wait()
+        y = lax.dot_general(c, held_ref[s].reshape(1024, 1024), nt, preferred_element_type=f32)
         for t in range(TILES):
             msgs[s][24 * t : 24 * t + 24, :] = y[0:24, 128 * t : 128 * t + 128]
             msgs[s][192 + t : 193 + t, :] = y[24:25, 128 * t : 128 * t + 128]
@@ -120,21 +115,20 @@
     pay_ref[...] = jnp.broadcast_to(jnp.concatenate(pay, axis=1)[None], pay_ref.shape)
 
 
-def sum_kernel(y0, y1, y2, y3, y_ref, gk_ref):
+def finish_kernel(y0, y1, y2, y3, x_ref, y_ref, out_ref, held_ref, sem):
     def total(at):
         return (y0[at, :] + y1[at, :]) + (y2[at, :] + y3[at, :])
 
     for t in range(TILES):
         s = total(slice(24 * t, 24 * t + 24))
-        y_ref[pl.ds(2 * t, 24, stride=16), :] = s[:, 0:64]
-        y_ref[pl.ds(2 * t + 1, 24, stride=16), :] = s[:, 64:128]
+        held_ref[pl.ds(2 * t, 24, stride=16), :] = s[:, 0:64]
+        held_ref[pl.ds(2 * t + 1, 24, stride=16), :] = s[:, 64:128]
     s = total(slice(192, 200))
-    y_ref[pl.ds(384, 8, stride=2), :] = s[:, 0:64]
-    y_ref[pl.ds(385, 8, stride=2), :] = s[:, 64:128]
-    gk_ref[...] = total(slice(BODY, MSG))
-
-
-def solve_kernel(x_ref, gk_ref, out_ref):
+    held_ref[pl.ds(384, 8, stride=2), :] = s[:, 0:64]
+    held_ref[pl.ds(385, 8, stride=2), :] = s[:, 64:128]
+    copy = pltpu.make_async_copy(held_ref, y_ref, sem)
+    copy.start()
+    gram_k = unfold(total(slice(BODY, MSG)))
     x = jnp.sum(x_ref[...].reshape(16, 4, 4, 128), axis=0)
     d = jnp.concatenate([x[q][:, 96 : 96 + R] for q in range(4)], axis=0)
     x = (x[0] + x[1]) + (x[2] + x[3])
@@ -153,7 +147,7 @@
         gram = jnp.where(apart == q, d[q : q + 1, :], gram)
     gram = gram + transposed(gram)
     gram = jnp.where(apart == 0, d[0:1, :], gram)
-    n = jnp.where((row < R) & (lane < R), gram * unfold(gk_ref[...]), 0.0)
+    n = jnp.where((row < R) & (lane < R), gram * gram_k, 0.0)
     a = jnp.concatenate([n, m, jnp.zeros((32, 80), f32)], axis=1)
     row_at = sublanes_of((32, 128))
     for first in range(0, R, BLOCK):
@@ -169,16 +163,17 @@
             a = eliminate(a)
             cols[q + 1 :] = [eliminate(x) for x in cols[q + 1 :]]
     out_ref[...] = pad_rows(a, 128).T[32:48, 0:R]
-
-
-def call(kernel, out, specs, flops=0, nbytes=0, scratch=()):
+    copy.wait()
+
+
+def call(kernel, out, specs, flops=0, nbytes=0, scratch=(), out_specs=None):
     return pl.pallas_call(
         kernel,
         out_shape=out,
         in_specs=specs,
-        out_specs=jax.tree.map(lambda _: VM, out),
+        out_specs=out_specs or jax.tree.map(lambda _: VM, out),
         scratch_shapes=scratch,
-        compiler_params=pltpu.CompilerParams(vmem_limit_bytes=10 * 2**20),
+        compiler_params=pltpu.CompilerParams(vmem_limit_bytes=12 * 2**20),
         cost_estimate=pl.CostEstimate(flops=flops, bytes_accessed=nbytes, transcendentals=0),
     )
 
@@ -196,19 +191,19 @@
     js = [shift(j0, "ia", s, 4) for s in (1, 2, 3)]
     packed = call(pack_kernel, sds((16, 16, 128), bf16), [HB], scratch=[pltpu.VMEM((R, 64), bf16), dma(())])(factor_k)
     c = lax.all_to_all(packed, ("z", "c"), 0, 0, tiled=True)
-    part = call(load_kernel, sds((16, 64, 1024), bf16), [HB], 0, 2**22, [dma(())])(tensor)
-    part = pltpu.with_memory_space_constraint(part, pltpu.VMEM)
     b = call(factor_kernel, sds((40, 128), f32), [VM] * 4, 2**33, 2**20)(j0, *js)
     bs = [b] + [shift(b, "ka", 4 - s, 4) for s in (1, 2, 3)]
     msgs = call(
-        contract_kernel, [sds((MSG, 128), f32)] * 4, [VM, VM, HB], 2**34, 2**23,
-        [pltpu.VMEM((3, 16, 64, 1024), bf16), dma((3,))],
-    )(c, part, tensor)
+        contract_kernel, [sds((MSG, 128), f32)] * 4, [VM, HB], 2**34, 2**23,
+        [pltpu.VMEM((4, 16, 64, 1024), bf16), dma((4,))],
+    )(c, tensor)
     got = [shift(msgs[s], "ka", s, 4) for s in (1, 2, 3)]
     pay = call(partial_kernel, sds((64, 4, 128), f32), [VM] * 8)(*msgs, *bs)
     pay = lax.all_to_all(pay, ("z", "c", "ka"), 0, 0, tiled=True)
-    y, gram_k = call(sum_kernel, [sds((400, 64), f32), sds((8, 128), f32)], [VM] * 4, 0, 2**21)(msgs[0], *got)
-    new_factor = call(solve_kernel, sds((16, R), f32), [VM] * 2)(pay, gram_k)
+    y, new_factor = call(
+        finish_kernel, [sds((400, 64), f32), sds((16, R), f32)], [VM] * 5, 0, 0,
+        [pltpu.VMEM((400, 64), f32), dma(())], [HB, VM],
+    )(msgs[0], *got, pay)
     return y.reshape(R, 16, 64), new_factor.T
 
 

time: 52 us -> 49.7 us (0.956)
  Pallas kernels: 10.8 us -> 9.14 us
  starting transfers between devices: 32.8 us -> 31.3 us
  local copies, waits for them, and re-layouts: 0.01 us -> 0.68 us
    pallas_call x4 -> x2, Pallas kernels: 8.28 us -> 6.58 us  [the longest x1 4.53 us: per_device(): call(contract_kernel, [sds((MSG, 128), f32)] * 4, [VM, HB], 2 ** 34, 2 **...]
    all_to_all x1, starting transfers between devices: 8.15 us -> 6.67 us  [per_device(): pay = lax.all_to_all(pay, ('z', 'c', 'ka'), 0, 0, tiled=True)]
    unnamed x2, local copies, waits for them, and re-layouts: 0.01 us -> 0.68 us
  transfers between devices with their start and end apart: 11 -> 11, of which waited for: 3 -> 3; matrix products, arithmetic and copies ran while one was open for 0% -> 0% of each run, Pallas kernels for 17% -> 13%
where the time goes in v1:
time: 49.7 us; the launch traced here: 48.9 us
  starting transfers between devices  31.3 us (63%)
  Pallas kernels  9.14 us (18%)
  waiting for transfers between devices  7.13 us (14%)
  between operations  0.71 us (1%)
  local copies, waits for them, and re-layouts  0.68 us (1%)
    ppermute x9, starting transfers between devices, shift(): return lax.ppermute(x, axis, [(i, (i + by) % n) for i in range(n)])  14.6 us
    all_to_all x1, starting transfers between devices, per_device(): c = lax.all_to_all(packed, ('z', 'c'), 0, 0, tiled=True)  10 us
    all_to_all x1, starting transfers between devices, per_device(): pay = lax.all_to_all(pay, ('z', 'c', 'ka'), 0, 0, tiled=True)  6.67 us
    ppermute x9, waiting for transfers between devices, shift(): return lax.ppermute(x, axis, [(i, (i + by) % n) for i in range(n)])  5.18 us
    pallas_call x1, Pallas kernels, per_device(): call(contract_kernel, [sds((MSG, 128), f32)] * 4, [VM, HB], 2 ** 34, 2 **...  4.53 us
    pallas_call x1, Pallas kernels, per_device(): call(finish_kernel, [sds((400, 64), f32), sds((16, R), f32)], [VM] * 5, 0...  2.05 us
    all_to_all x1, waiting for transfers between devices, per_device(): c = lax.all_to_all(packed, ('z', 'c'), 0, 0, tiled=True)  1.95 us
    pallas_call x1, Pallas kernels, per_device(): call(pack_kernel, sds((16, 16, 128), bf16), [HB], scratch=[pltpu.VMEM((R,...  1.41 us
  transfers between devices with their start and end apart: 11, of which 3 were waited for; matrix products, arithmetic and copies ran while one was open for 0% of the time, Pallas kernels for 13%

profile of v1, /device:TPU:1, one launch (start us, length us, event | category | flops | bytes accessed | tf_op | source)
XLA Modules:
  0.0 48.9 jit_solution(11665660244574634279)
XLA Ops:
  0.6 3.6 %collective-permute-start.5 = (bf16[16,25]{1,0:T(8,128)(2,1)}, bf16[16,25]{1,0:T(8,128)(2,1)S(1)}, u32[]{:S(2)}, u32[]{:S(2)}) collective-permute-start(bf16[16,25]{1,0:T(8,128)(2,1)} %bitcast.3), channel_id=1, source_target_pairs={{0,192},{64,0},{128,64},{192,128},{1,193},{65,1},{129,65},{193,129... | collective-permute-start | bytes 2408 | tf_op jit(solution)/shard_map/ppermute | solution.py:182
  4.3 0.3 collective-permute-start.4
  4.6 0.7 %collective-permute-start.3 = (bf16[16,25]{1,0:T(8,128)(2,1)}, bf16[16,25]{1,0:T(8,128)(2,1)S(1)}, u32[]{:S(2)}, u32[]{:S(2)}) collective-permute-start(bf16[16,25]{1,0:T(8,128)(2,1)} %bitcast.5), channel_id=1, source_target_pairs={{0,64},{64,128},{128,192},{192,0},{1,65},{65,129},{129,193},{193,1... | collective-permute-start | bytes 2408 | tf_op jit(solution)/shard_map/ppermute | solution.py:182
  5.3 1.4 %shard_map.50 = bf16[16,16,128]{2,1,0:T(8,128)(2,1)} custom-call(bf16[25,64]{1,0:T(8,128)(2,1)} %k_ref.1), custom_call_target="tpu_custom_call" | custom-call | tf_op jit(solution)/shard_map/pallas_call | solution.py:192
  6.7 10.0 %all-to-all-start = ((bf16[16,16,128]{2,1,0:T(8,128)(2,1)}), bf16[16,16,128]{2,1,0:T(8,128)(2,1)S(1)}, u32[]{:S(2)}, u32[]{:S(2)}) async-start(bf16[16,16,128]{2,1,0:T(8,128)(2,1)} %shard_map.50), calls=%async_computation | async-start | bytes 131072 | tf_op jit(solution)/shard_map/all_to_all | solution.py:193
  16.7 0.0 collective-permute-done.5.j3
  16.7 0.0 collective-permute-done.4.j2
  16.8 0.0 collective-permute-done.3.j1
  16.8 0.0 copy-start
  16.8 0.7 %copy-done = bf16[25,16]{0,1:T(8,128)(2,1)S(1)} copy-done((bf16[25,16]{0,1:T(8,128)(2,1)S(1)}, bf16[25,16]{0,1:T(8,128)(2,1)}, u32[]{:S(2)}) %copy-start) | copy-done | bytes 824
  17.5 0.3 shard_map.52.b0
  17.7 1.3 %collective-permute-start.8 = (f32[40,128]{1,0:T(8,128)S(1)}, f32[40,128]{1,0:T(8,128)S(1)}, u32[]{:S(2)}, u32[]{:S(2)}) collective-permute-start(f32[40,128]{1,0:T(8,128)S(1)} %shard_map.52.b0), channel_id=1, source_target_pairs={{0,1},{1,2},{2,3},{3,0},{4,5},{5,6},{6,7},{7,4},{8,9},{9,10},{10,1... | collective-permute-start | bytes 61448 | tf_op jit(solution)/shard_map/ppermute | solution.py:182
  19.0 2.5 %collective-permute-start.7 = (f32[40,128]{1,0:T(8,128)S(1)}, f32[40,128]{1,0:T(8,128)S(1)}, u32[]{:S(2)}, u32[]{:S(2)}) collective-permute-start(f32[40,128]{1,0:T(8,128)S(1)} %shard_map.52.b0), channel_id=1, source_target_pairs={{0,2},{1,3},{2,0},{3,1},{4,6},{5,7},{6,4},{7,5},{8,10},{9,11},{10,... | collective-permute-start | bytes 61448 | tf_op jit(solution)/shard_map/ppermute | solution.py:182
  21.4 1.2 %collective-permute-start.6 = (f32[40,128]{1,0:T(8,128)S(1)}, f32[40,128]{1,0:T(8,128)S(1)}, u32[]{:S(2)}, u32[]{:S(2)}) collective-permute-start(f32[40,128]{1,0:T(8,128)S(1)} %shard_map.52.b0), channel_id=1, source_target_pairs={{0,3},{1,0},{2,1},{3,2},{4,7},{5,4},{6,5},{7,6},{8,11},{9,8},{10,9... | collective-permute-start | bytes 61448 | tf_op jit(solution)/shard_map/ppermute | solution.py:182
  22.6 2.0 %all-to-all-done.c_ref = bf16[16,16,128]{2,1,0:T(8,128)(2,1)S(1)} async-done(((bf16[16,16,128]{2,1,0:T(8,128)(2,1)}), bf16[16,16,128]{2,1,0:T(8,128)(2,1)S(1)}, u32[]{:S(2)}, u32[]{:S(2)}) %all-to-all-start) | async-done | bytes 65568 | tf_op jit(solution)/shard_map/all_to_all | solution.py:193
  24.5 4.5 %shard_map.51 = (f32[208,128]{1,0:T(8,128)S(1)}, f32[208,128]{1,0:T(8,128)S(1)}, f32[208,128]{1,0:T(8,128)S(1)}, f32[208,128]{1,0:T(8,128)S(1)}) custom-call(bf16[16,16,128]{2,1,0:T(8,128)(2,1)S(1)} %all-to-all-done.c_ref, bf16[16,256,1024]{2,1,0:T(8,128)(2,1)} %t_ref.1), custom_call_target="tpu_custom_call" | custom-call | flops 17179869184 | bytes 8388608 | tf_op jit(solution)/shard_map/pallas_call | solution.py:196
  29.1 0.0 collective-permute-done.8.b3
  29.1 0.0 collective-permute-done.7.b2
  29.1 0.0 collective-permute-done.6.b1
  29.1 0.9 %shard_map.53 = f32[64,4,128]{2,1,0:T(4,128)} custom-call(f32[208,128]{1,0:T(8,128)S(1)} %get-tuple-element.8.y0, f32[208,128]{1,0:T(8,128)S(1)} %get-tuple-element.9.y1, f32[208,128]{1,0:T(8,128)S(1)} %get-tuple-element.10.y2, f32[208,128]{1,0:T(8,128)S(1)} %get-tuple-element.11.y3, f32[40,128]{1,0:T(8,128)S(1)} %shard_map.52.b0, ...), custom_call_target="tpu_custom_call" | custom-call | tf_op jit(solution)/shard_map/pallas_call | solution.py:201
  30.0 6.7 %all-to-all-start.1 = ((f32[64,4,128]{2,1,0:T(4,128)}), f32[64,4,128]{2,1,0:T(4,128)S(1)}, u32[]{:S(2)}, u32[]{:S(2)}) async-start(f32[64,4,128]{2,1,0:T(4,128)} %shard_map.53), calls=%async_computation.1 | async-start | bytes 262144 | tf_op jit(solution)/shard_map/all_to_all | solution.py:202
  36.7 1.5 %collective-permute-start = (f32[208,128]{1,0:T(8,128)S(1)}, f32[208,128]{1,0:T(8,128)S(1)}, u32[]{:S(2)}, u32[]{:S(2)}) collective-permute-start(f32[208,128]{1,0:T(8,128)S(1)} %get-tuple-element.9.y1), channel_id=1, source_target_pairs={{0,1},{1,2},{2,3},{3,0},{4,5},{5,6},{6,7},{7,4},{8,9},{9,10},{10,1... | collective-permute-start | bytes 319496 | tf_op jit(solution)/shard_map/ppermute | solution.py:182
  38.1 2.4 %collective-permute-start.1 = (f32[208,128]{1,0:T(8,128)S(1)}, f32[208,128]{1,0:T(8,128)S(1)}, u32[]{:S(2)}, u32[]{:S(2)}) collective-permute-start(f32[208,128]{1,0:T(8,128)S(1)} %get-tuple-element.10.y2), channel_id=1, source_target_pairs={{0,2},{1,3},{2,0},{3,1},{4,6},{5,7},{6,4},{7,5},{8,10},{9,11},{10,... | collective-permute-start | bytes 319496 | tf_op jit(solution)/shard_map/ppermute | solution.py:182
  40.5 1.2 %collective-permute-start.2 = (f32[208,128]{1,0:T(8,128)S(1)}, f32[208,128]{1,0:T(8,128)S(1)}, u32[]{:S(2)}, u32[]{:S(2)}) collective-permute-start(f32[208,128]{1,0:T(8,128)S(1)} %get-tuple-element.11.y3), channel_id=1, source_target_pairs={{0,3},{1,0},{2,1},{3,2},{4,7},{5,4},{6,5},{7,6},{8,11},{9,8},{10,9... | collective-permute-start | bytes 319496 | tf_op jit(solution)/shard_map/ppermute | solution.py:182
  41.7 0.8 %collective-permute-done.y1 = f32[208,128]{1,0:T(8,128)S(1)} collective-permute-done((f32[208,128]{1,0:T(8,128)S(1)}, f32[208,128]{1,0:T(8,128)S(1)}, u32[]{:S(2)}, u32[]{:S(2)}) %collective-permute-start) | collective-permute-done | bytes 106528 | tf_op jit(solution)/shard_map/ppermute | solution.py:182
  42.5 4.3 %collective-permute-done.1.y2 = f32[208,128]{1,0:T(8,128)S(1)} collective-permute-done((f32[208,128]{1,0:T(8,128)S(1)}, f32[208,128]{1,0:T(8,128)S(1)}, u32[]{:S(2)}, u32[]{:S(2)}) %collective-permute-start.1) | collective-permute-done | bytes 106528 | tf_op jit(solution)/shard_map/ppermute | solution.py:182
  46.9 0.0 collective-permute-done.2.y3
  46.9 0.0 all-to-all-done.1.x_ref
  46.9 2.1 %shard_map.54 = (f32[400,64]{1,0:T(8,128)}, f32[16,25]{1,0:T(8,128)}) custom-call(f32[208,128]{1,0:T(8,128)S(1)} %get-tuple-element.8.y0, f32[208,128]{1,0:T(8,128)S(1)} %collective-permute-done.y1, f32[208,128]{1,0:T(8,128)S(1)} %collective-permute-done.1.y2, f32[208,128]{1,0:T(8,128)S(1)} %collective-permute-done.2.y3, f32[64,4,128]{2,1,0:T(4,128)S(1)} %all-to-all-done.1.x_ref), custom_call_target="tpu_custom_call" | custom-call | tf_op jit(solution)/shard_map/pallas_call | solution.py:203
Async XLA Ops:
  0.6 16.1 %collective-permute-start.5 = (bf16[16,25]{1,0:T(8,128)(2,1)}, bf16[16,25]{1,0:T(8,128)(2,1)S(1)}, u32[]{:S(2)}, u32[]{:S(2)}) collective-permute-start(bf16[16,25]{1,0:T(8,128)(2,1)} %bitcast.3), channel_id=1, source_target_pairs={{0,192},{64,0},{128,64},{192,128},{1,193},{65,1},{129,65},{193,129... | collective-permute-start | bytes 2408 | tf_op jit(solution)/shard_map/ppermute | solution.py:182
  4.3 12.5 %collective-permute-start.4 = (bf16[16,25]{1,0:T(8,128)(2,1)}, bf16[16,25]{1,0:T(8,128)(2,1)S(1)}, u32[]{:S(2)}, u32[]{:S(2)}) collective-permute-start(bf16[16,25]{1,0:T(8,128)(2,1)} %bitcast.4), channel_id=1, source_target_pairs={{0,128},{64,192},{128,0},{192,64},{1,129},{65,193},{129,1},{193,65... | collective-permute-start | bytes 2408 | tf_op jit(solution)/shard_map/ppermute | solution.py:182
  4.6 12.1 %collective-permute-start.3 = (bf16[16,25]{1,0:T(8,128)(2,1)}, bf16[16,25]{1,0:T(8,128)(2,1)S(1)}, u32[]{:S(2)}, u32[]{:S(2)}) collective-permute-start(bf16[16,25]{1,0:T(8,128)(2,1)} %bitcast.5), channel_id=1, source_target_pairs={{0,64},{64,128},{128,192},{192,0},{1,65},{65,129},{129,193},{193,1... | collective-permute-start | bytes 2408 | tf_op jit(solution)/shard_map/ppermute | solution.py:182
  6.7 17.8 %all-to-all-start = ((bf16[16,16,128]{2,1,0:T(8,128)(2,1)}), bf16[16,16,128]{2,1,0:T(8,128)(2,1)S(1)}, u32[]{:S(2)}, u32[]{:S(2)}) async-start(bf16[16,16,128]{2,1,0:T(8,128)(2,1)} %shard_map.50), calls=%async_computation | async-start | bytes 131072 | tf_op jit(solution)/shard_map/all_to_all | solution.py:193
  16.8 0.7 %copy-start = (bf16[25,16]{0,1:T(8,128)(2,1)S(1)}, bf16[25,16]{0,1:T(8,128)(2,1)}, u32[]{:S(2)}) copy-start(bf16[25,16]{0,1:T(8,128)(2,1)} %param.4) | copy-start | bytes 2404
  17.7 11.4 %collective-permute-start.8 = (f32[40,128]{1,0:T(8,128)S(1)}, f32[40,128]{1,0:T(8,128)S(1)}, u32[]{:S(2)}, u32[]{:S(2)}) collective-permute-start(f32[40,128]{1,0:T(8,128)S(1)} %shard_map.52.b0), channel_id=1, source_target_pairs={{0,1},{1,2},{2,3},{3,0},{4,5},{5,6},{6,7},{7,4},{8,9},{9,10},{10,1... | collective-permute-start | bytes 61448 | tf_op jit(solution)/shard_map/ppermute | solution.py:182
  19.0 10.1 %collective-permute-start.7 = (f32[40,128]{1,0:T(8,128)S(1)}, f32[40,128]{1,0:T(8,128)S(1)}, u32[]{:S(2)}, u32[]{:S(2)}) collective-permute-start(f32[40,128]{1,0:T(8,128)S(1)} %shard_map.52.b0), channel_id=1, source_target_pairs={{0,2},{1,3},{2,0},{3,1},{4,6},{5,7},{6,4},{7,5},{8,10},{9,11},{10,... | collective-permute-start | bytes 61448 | tf_op jit(solution)/shard_map/ppermute | solution.py:182
  21.4 7.7 %collective-permute-start.6 = (f32[40,128]{1,0:T(8,128)S(1)}, f32[40,128]{1,0:T(8,128)S(1)}, u32[]{:S(2)}, u32[]{:S(2)}) collective-permute-start(f32[40,128]{1,0:T(8,128)S(1)} %shard_map.52.b0), channel_id=1, source_target_pairs={{0,3},{1,0},{2,1},{3,2},{4,7},{5,4},{6,5},{7,6},{8,11},{9,8},{10,9... | collective-permute-start | bytes 61448 | tf_op jit(solution)/shard_map/ppermute | solution.py:182
  30.0 16.9 %all-to-all-start.1 = ((f32[64,4,128]{2,1,0:T(4,128)}), f32[64,4,128]{2,1,0:T(4,128)S(1)}, u32[]{:S(2)}, u32[]{:S(2)}) async-start(f32[64,4,128]{2,1,0:T(4,128)} %shard_map.53), calls=%async_computation.1 | async-start | bytes 262144 | tf_op jit(solution)/shard_map/all_to_all | solution.py:202
  36.7 5.9 %collective-permute-start = (f32[208,128]{1,0:T(8,128)S(1)}, f32[208,128]{1,0:T(8,128)S(1)}, u32[]{:S(2)}, u32[]{:S(2)}) collective-permute-start(f32[208,128]{1,0:T(8,128)S(1)} %get-tuple-element.9.y1), channel_id=1, source_target_pairs={{0,1},{1,2},{2,3},{3,0},{4,5},{5,6},{6,7},{7,4},{8,9},{9,10},{10,1... | collective-permute-start | bytes 319496 | tf_op jit(solution)/shard_map/ppermute | solution.py:182
  38.1 8.7 %collective-permute-start.1 = (f32[208,128]{1,0:T(8,128)S(1)}, f32[208,128]{1,0:T(8,128)S(1)}, u32[]{:S(2)}, u32[]{:S(2)}) collective-permute-start(f32[208,128]{1,0:T(8,128)S(1)} %get-tuple-element.10.y2), channel_id=1, source_target_pairs={{0,2},{1,3},{2,0},{3,1},{4,6},{5,7},{6,4},{7,5},{8,10},{9,11},{10,... | collective-permute-start | bytes 319496 | tf_op jit(solution)/shard_map/ppermute | solution.py:182
  40.5 6.3 %collective-permute-start.2 = (f32[208,128]{1,0:T(8,128)S(1)}, f32[208,128]{1,0:T(8,128)S(1)}, u32[]{:S(2)}, u32[]{:S(2)}) collective-permute-start(f32[208,128]{1,0:T(8,128)S(1)} %get-tuple-element.11.y3), channel_id=1, source_target_pairs={{0,3},{1,0},{2,1},{3,2},{4,7},{5,4},{6,5},{7,6},{8,11},{9,8},{10,9... | collective-permute-start | bytes 319496 | tf_op jit(solution)/shard_map/ppermute | solution.py:182

commit v2 on v1

--- a/solution.py
+++ b/solution.py
@@ -42,11 +42,16 @@
     return pad_rows(x, 128).T[0:rows, 0 : x.shape[0]]
 
 
-def pack_kernel(k_ref, out_ref, k_vmem, sem):
-    copy = pltpu.make_async_copy(k_ref, k_vmem, sem)
-    copy.start()
-    copy.wait()
-    k = pad_rows(k_vmem[...].astype(f32), 32)
+def own_kernel(k_ref, j_ref, kout_ref, jout_ref, sems):
+    copies = [pltpu.make_async_copy(k_ref, kout_ref, sems.at[0]), pltpu.make_async_copy(j_ref, jout_ref, sems.at[1])]
+    for copy in copies:
+        copy.start()
+    for copy in copies:
+        copy.wait()
+
+
+def pack_kernel(k_ref, out_ref):
+    k = pad_rows(k_ref[...].astype(f32), 32)
     folded = jnp.concatenate([k[0:16], k[16:32]], axis=1).astype(bf16)
     out_ref[...] = jnp.broadcast_to(folded[None], out_ref.shape)
 
@@ -189,21 +194,24 @@
     tensor = pltpu.with_memory_space_constraint(tensor, pltpu.HBM)
     j0 = factor_j.T
     js = [shift(j0, "ia", s, 4) for s in (1, 2, 3)]
-    packed = call(pack_kernel, sds((16, 16, 128), bf16), [HB], scratch=[pltpu.VMEM((R, 64), bf16), dma(())])(factor_k)
+    k_own, j_own = call(
+        own_kernel, [sds((R, 64), bf16), sds((16, R), bf16)], [HB, HB], 0, 0, [dma((2,))]
+    )(factor_k, pltpu.with_memory_space_constraint(j0, pltpu.HBM))
+    packed = call(pack_kernel, sds((16, 16, 128), bf16), [VM])(k_own)
     c = lax.all_to_all(packed, ("z", "c"), 0, 0, tiled=True)
-    b = call(factor_kernel, sds((40, 128), f32), [VM] * 4, 2**33, 2**20)(j0, *js)
+    b = call(factor_kernel, sds((40, 128), f32), [VM] * 4, 2**33, 2**20)(j_own, *js)
     bs = [b] + [shift(b, "ka", 4 - s, 4) for s in (1, 2, 3)]
     msgs = call(
         contract_kernel, [sds((MSG, 128), f32)] * 4, [VM, HB], 2**34, 2**23,
         [pltpu.VMEM((4, 16, 64, 1024), bf16), dma((4,))],
     )(c, tensor)
-    got = [shift(msgs[s], "ka", s, 4) for s in (1, 2, 3)]
+    got = {s: shift(msgs[s], "ka", s, 4) for s in (2, 1, 3)}
     pay = call(partial_kernel, sds((64, 4, 128), f32), [VM] * 8)(*msgs, *bs)
     pay = lax.all_to_all(pay, ("z", "c", "ka"), 0, 0, tiled=True)
     y, new_factor = call(
         finish_kernel, [sds((400, 64), f32), sds((16, R), f32)], [VM] * 5, 0, 0,
         [pltpu.VMEM((400, 64), f32), dma(())], [HB, VM],
-    )(msgs[0], *got, pay)
+    )(msgs[0], got[2], got[1], got[3], pay)
     return y.reshape(R, 16, 64), new_factor.T
 
 

time: 49.7 us -> 49 us (0.986)
  the two profiles are of different devices: /device:TPU:1 before, /device:TPU:8 now
where the time goes in v2:
time: 49 us; the launch traced here: 48.7 us
  starting transfers between devices  31.9 us (65%)
  Pallas kernels  9.18 us (19%)
  waiting for transfers between devices  6.86 us (14%)
  between operations  0.72 us (1%)
    ppermute x9, starting transfers between devices, shift(): return lax.ppermute(x, axis, [(i, (i + by) % n) for i in range(n)])  17.1 us
    all_to_all x1, starting transfers between devices, per_device(): c = lax.all_to_all(packed, ('z', 'c'), 0, 0, tiled=True)  8.57 us
    all_to_all x1, starting transfers between devices, per_device(): pay = lax.all_to_all(pay, ('z', 'c', 'ka'), 0, 0, tiled=True)  6.27 us
    pallas_call x1, Pallas kernels, per_device(): call(contract_kernel, [sds((MSG, 128), f32)] * 4, [VM, HB], 2 ** 34, 2 **...  4.53 us
    ppermute x9, waiting for transfers between devices, shift(): return lax.ppermute(x, axis, [(i, (i + by) % n) for i in range(n)])  3.83 us
    pallas_call x1, Pallas kernels, per_device(): call(finish_kernel, [sds((400, 64), f32), sds((16, R), f32)], [VM] * 5, 0...  2.05 us
    all_to_all x1, waiting for transfers between devices, per_device(): c = lax.all_to_all(packed, ('z', 'c'), 0, 0, tiled=True)  1.88 us
    all_to_all x1, waiting for transfers between devices, per_device(): pay = lax.all_to_all(pay, ('z', 'c', 'ka'), 0, 0, tiled=True)  1.15 us
  transfers between devices with their start and end apart: 11, of which 4 were waited for; matrix products, arithmetic and copies ran while one was open for 0% of the time, Pallas kernels for 13%

profile of v2, /device:TPU:8, one launch (start us, length us, event | category | flops | bytes accessed | tf_op | source)
XLA Modules:
  0.0 48.7 jit_solution(14596349323408361755)
XLA Ops:
  0.6 2.3 %collective-permute-start.5 = (bf16[16,25]{1,0:T(8,128)(2,1)}, bf16[16,25]{1,0:T(8,128)(2,1)S(1)}, u32[]{:S(2)}, u32[]{:S(2)}) collective-permute-start(bf16[16,25]{1,0:T(8,128)(2,1)} %bitcast.3), channel_id=1, source_target_pairs={{0,192},{64,0},{128,64},{192,128},{1,193},{65,1},{129,65},{193,129... | collective-permute-start | bytes 2408 | tf_op jit(solution)/shard_map/ppermute | solution.py:187
  2.9 0.9 %collective-permute-start.4 = (bf16[16,25]{1,0:T(8,128)(2,1)}, bf16[16,25]{1,0:T(8,128)(2,1)S(1)}, u32[]{:S(2)}, u32[]{:S(2)}) collective-permute-start(bf16[16,25]{1,0:T(8,128)(2,1)} %bitcast.4), channel_id=1, source_target_pairs={{0,128},{64,192},{128,0},{192,64},{1,129},{65,193},{129,1},{193,65... | collective-permute-start | bytes 2408 | tf_op jit(solution)/shard_map/ppermute | solution.py:187
  3.7 1.9 %collective-permute-start.3 = (bf16[16,25]{1,0:T(8,128)(2,1)}, bf16[16,25]{1,0:T(8,128)(2,1)S(1)}, u32[]{:S(2)}, u32[]{:S(2)}) collective-permute-start(bf16[16,25]{1,0:T(8,128)(2,1)} %bitcast.5), channel_id=1, source_target_pairs={{0,64},{64,128},{128,192},{192,0},{1,65},{65,129},{129,193},{193,1... | collective-permute-start | bytes 2408 | tf_op jit(solution)/shard_map/ppermute | solution.py:187
  5.6 0.7 %shard_map.50 = (bf16[25,64]{1,0:T(8,128)(2,1)S(1)}, bf16[16,25]{1,0:T(8,128)(2,1)S(1)}) custom-call(bf16[25,64]{1,0:T(8,128)(2,1)} %k_ref.1, bf16[16,25]{1,0:T(8,128)(2,1)} %bitcast.6), custom_call_target="tpu_custom_call" | custom-call | tf_op jit(solution)/shard_map/pallas_call | solution.py:197
  6.4 0.7 %shard_map.51 = bf16[16,16,128]{2,1,0:T(8,128)(2,1)} custom-call(bf16[25,64]{1,0:T(8,128)(2,1)S(1)} %get-tuple-element.10.k_ref), custom_call_target="tpu_custom_call" | custom-call | tf_op jit(solution)/shard_map/pallas_call | solution.py:200
  7.1 8.6 %all-to-all-start = ((bf16[16,16,128]{2,1,0:T(8,128)(2,1)}), bf16[16,16,128]{2,1,0:T(8,128)(2,1)S(1)}, u32[]{:S(2)}, u32[]{:S(2)}) async-start(bf16[16,16,128]{2,1,0:T(8,128)(2,1)} %shard_map.51), calls=%async_computation | async-start | bytes 131072 | tf_op jit(solution)/shard_map/all_to_all | solution.py:201
  15.7 0.0 collective-permute-done.5.j3
  15.7 0.0 collective-permute-done.4.j2
  15.7 0.0 collective-permute-done.3.j1
  15.7 0.3 shard_map.53.b0
  16.0 1.5 %collective-permute-start.8 = (f32[40,128]{1,0:T(8,128)S(1)}, f32[40,128]{1,0:T(8,128)S(1)}, u32[]{:S(2)}, u32[]{:S(2)}) collective-permute-start(f32[40,128]{1,0:T(8,128)S(1)} %shard_map.53.b0), channel_id=1, source_target_pairs={{0,1},{1,2},{2,3},{3,0},{4,5},{5,6},{6,7},{7,4},{8,9},{9,10},{10,1... | collective-permute-start | bytes 61448 | tf_op jit(solution)/shard_map/ppermute | solution.py:187
  17.5 2.7 %collective-permute-start.7 = (f32[40,128]{1,0:T(8,128)S(1)}, f32[40,128]{1,0:T(8,128)S(1)}, u32[]{:S(2)}, u32[]{:S(2)}) collective-permute-start(f32[40,128]{1,0:T(8,128)S(1)} %shard_map.53.b0), channel_id=1, source_target_pairs={{0,2},{1,3},{2,0},{3,1},{4,6},{5,7},{6,4},{7,5},{8,10},{9,11},{10,... | collective-permute-start | bytes 61448 | tf_op jit(solution)/shard_map/ppermute | solution.py:187
  20.2 1.4 %collective-permute-start.6 = (f32[40,128]{1,0:T(8,128)S(1)}, f32[40,128]{1,0:T(8,128)S(1)}, u32[]{:S(2)}, u32[]{:S(2)}) collective-permute-start(f32[40,128]{1,0:T(8,128)S(1)} %shard_map.53.b0), channel_id=1, source_target_pairs={{0,3},{1,0},{2,1},{3,2},{4,7},{5,4},{6,5},{7,6},{8,11},{9,8},{10,9... | collective-permute-start | bytes 61448 | tf_op jit(solution)/shard_map/ppermute | solution.py:187
  21.7 1.9 %all-to-all-done.c_ref = bf16[16,16,128]{2,1,0:T(8,128)(2,1)S(1)} async-done(((bf16[16,16,128]{2,1,0:T(8,128)(2,1)}), bf16[16,16,128]{2,1,0:T(8,128)(2,1)S(1)}, u32[]{:S(2)}, u32[]{:S(2)}) %all-to-all-start) | async-done | bytes 65568 | tf_op jit(solution)/shard_map/all_to_all | solution.py:201
  23.5 4.5 %shard_map.52 = (f32[208,128]{1,0:T(8,128)S(1)}, f32[208,128]{1,0:T(8,128)S(1)}, f32[208,128]{1,0:T(8,128)S(1)}, f32[208,128]{1,0:T(8,128)S(1)}) custom-call(bf16[16,16,128]{2,1,0:T(8,128)(2,1)S(1)} %all-to-all-done.c_ref, bf16[16,256,1024]{2,1,0:T(8,128)(2,1)} %t_ref.1), custom_call_target="tpu_custom_call" | custom-call | flops 17179869184 | bytes 8388608 | tf_op jit(solution)/shard_map/pallas_call | solution.py:204
  28.1 0.0 collective-permute-done.8.b3
  28.1 0.0 collective-permute-done.7.b2
  28.1 0.0 collective-permute-done.6.b1
  28.1 0.9 %shard_map.54 = f32[64,4,128]{2,1,0:T(4,128)} custom-call(f32[208,128]{1,0:T(8,128)S(1)} %get-tuple-element.11.y0, f32[208,128]{1,0:T(8,128)S(1)} %get-tuple-element.13.y1, f32[208,128]{1,0:T(8,128)S(1)} %get-tuple-element.12.y2, f32[208,128]{1,0:T(8,128)S(1)} %get-tuple-element.14.y3, f32[40,128]{1,0:T(8,128)S(1)} %shard_map.53.b0, ...), custom_call_target="tpu_custom_call" | custom-call | tf_op jit(solution)/shard_map/pallas_call | solution.py:209
  29.0 6.3 %all-to-all-start.1 = ((f32[64,4,128]{2,1,0:T(4,128)}), f32[64,4,128]{2,1,0:T(4,128)S(1)}, u32[]{:S(2)}, u32[]{:S(2)}) async-start(f32[64,4,128]{2,1,0:T(4,128)} %shard_map.54), calls=%async_computation.1 | async-start | bytes 262144 | tf_op jit(solution)/shard_map/all_to_all | solution.py:210
  35.3 3.2 %collective-permute-start = (f32[208,128]{1,0:T(8,128)S(1)}, f32[208,128]{1,0:T(8,128)S(1)}, u32[]{:S(2)}, u32[]{:S(2)}) collective-permute-start(f32[208,128]{1,0:T(8,128)S(1)} %get-tuple-element.12.y2), channel_id=1, source_target_pairs={{0,2},{1,3},{2,0},{3,1},{4,6},{5,7},{6,4},{7,5},{8,10},{9,11},{10,... | collective-permute-start | bytes 319496 | tf_op jit(solution)/shard_map/ppermute | solution.py:187
  38.4 0.6 %collective-permute-start.1 = (f32[208,128]{1,0:T(8,128)S(1)}, f32[208,128]{1,0:T(8,128)S(1)}, u32[]{:S(2)}, u32[]{:S(2)}) collective-permute-start(f32[208,128]{1,0:T(8,128)S(1)} %get-tuple-element.13.y1), channel_id=1, source_target_pairs={{0,1},{1,2},{2,3},{3,0},{4,5},{5,6},{6,7},{7,4},{8,9},{9,10},{10,1... | collective-permute-start | bytes 319496 | tf_op jit(solution)/shard_map/ppermute | solution.py:187
  39.0 2.7 %collective-permute-start.2 = (f32[208,128]{1,0:T(8,128)S(1)}, f32[208,128]{1,0:T(8,128)S(1)}, u32[]{:S(2)}, u32[]{:S(2)}) collective-permute-start(f32[208,128]{1,0:T(8,128)S(1)} %get-tuple-element.14.y3), channel_id=1, source_target_pairs={{0,3},{1,0},{2,1},{3,2},{4,7},{5,4},{6,5},{7,6},{8,11},{9,8},{10,9... | collective-permute-start | bytes 319496 | tf_op jit(solution)/shard_map/ppermute | solution.py:187
  41.7 1.6 %collective-permute-done.y1 = f32[208,128]{1,0:T(8,128)S(1)} collective-permute-done((f32[208,128]{1,0:T(8,128)S(1)}, f32[208,128]{1,0:T(8,128)S(1)}, u32[]{:S(2)}, u32[]{:S(2)}) %collective-permute-start) | collective-permute-done | bytes 106528 | tf_op jit(solution)/shard_map/ppermute | solution.py:187
  43.3 2.2 %collective-permute-done.1.y2 = f32[208,128]{1,0:T(8,128)S(1)} collective-permute-done((f32[208,128]{1,0:T(8,128)S(1)}, f32[208,128]{1,0:T(8,128)S(1)}, u32[]{:S(2)}, u32[]{:S(2)}) %collective-permute-start.1) | collective-permute-done | bytes 106528 | tf_op jit(solution)/shard_map/ppermute | solution.py:187
  45.5 0.0 collective-permute-done.2.y3
  45.5 1.2 %all-to-all-done.1.x_ref = f32[64,4,128]{2,1,0:T(4,128)S(1)} async-done(((f32[64,4,128]{2,1,0:T(4,128)}), f32[64,4,128]{2,1,0:T(4,128)S(1)}, u32[]{:S(2)}, u32[]{:S(2)}) %all-to-all-start.1) | async-done | bytes 131104 | tf_op jit(solution)/shard_map/all_to_all | solution.py:210
  46.6 2.1 %shard_map.55 = (f32[400,64]{1,0:T(8,128)}, f32[16,25]{1,0:T(8,128)}) custom-call(f32[208,128]{1,0:T(8,128)S(1)} %get-tuple-element.11.y0, f32[208,128]{1,0:T(8,128)S(1)} %collective-permute-done.y1, f32[208,128]{1,0:T(8,128)S(1)} %collective-permute-done.1.y2, f32[208,128]{1,0:T(8,128)S(1)} %collective-permute-done.2.y3, f32[64,4,128]{2,1,0:T(4,128)S(1)} %all-to-all-done.1.x_ref), custom_call_target="tpu_custom_call" | custom-call | tf_op jit(solution)/shard_map/pallas_call | solution.py:211
Async XLA Ops:
  0.6 15.0 %collective-permute-start.5 = (bf16[16,25]{1,0:T(8,128)(2,1)}, bf16[16,25]{1,0:T(8,128)(2,1)S(1)}, u32[]{:S(2)}, u32[]{:S(2)}) collective-permute-start(bf16[16,25]{1,0:T(8,128)(2,1)} %bitcast.3), channel_id=1, source_target_pairs={{0,192},{64,0},{128,64},{192,128},{1,193},{65,1},{129,65},{193,129... | collective-permute-start | bytes 2408 | tf_op jit(solution)/shard_map/ppermute | solution.py:187
  2.9 12.8 %collective-permute-start.4 = (bf16[16,25]{1,0:T(8,128)(2,1)}, bf16[16,25]{1,0:T(8,128)(2,1)S(1)}, u32[]{:S(2)}, u32[]{:S(2)}) collective-permute-start(bf16[16,25]{1,0:T(8,128)(2,1)} %bitcast.4), channel_id=1, source_target_pairs={{0,128},{64,192},{128,0},{192,64},{1,129},{65,193},{129,1},{193,65... | collective-permute-start | bytes 2408 | tf_op jit(solution)/shard_map/ppermute | solution.py:187
  3.7 11.9 %collective-permute-start.3 = (bf16[16,25]{1,0:T(8,128)(2,1)}, bf16[16,25]{1,0:T(8,128)(2,1)S(1)}, u32[]{:S(2)}, u32[]{:S(2)}) collective-permute-start(bf16[16,25]{1,0:T(8,128)(2,1)} %bitcast.5), channel_id=1, source_target_pairs={{0,64},{64,128},{128,192},{192,0},{1,65},{65,129},{129,193},{193,1... | collective-permute-start | bytes 2408 | tf_op jit(solution)/shard_map/ppermute | solution.py:187
  7.1 16.4 %all-to-all-start = ((bf16[16,16,128]{2,1,0:T(8,128)(2,1)}), bf16[16,16,128]{2,1,0:T(8,128)(2,1)S(1)}, u32[]{:S(2)}, u32[]{:S(2)}) async-start(bf16[16,16,128]{2,1,0:T(8,128)(2,1)} %shard_map.51), calls=%async_computation | async-start | bytes 131072 | tf_op jit(solution)/shard_map/all_to_all | solution.py:201
  16.0 12.1 %collective-permute-start.8 = (f32[40,128]{1,0:T(8,128)S(1)}, f32[40,128]{1,0:T(8,128)S(1)}, u32[]{:S(2)}, u32[]{:S(2)}) collective-permute-start(f32[40,128]{1,0:T(8,128)S(1)} %shard_map.53.b0), channel_id=1, source_target_pairs={{0,1},{1,2},{2,3},{3,0},{4,5},{5,6},{6,7},{7,4},{8,9},{9,10},{10,1... | collective-permute-start | bytes 61448 | tf_op jit(solution)/shard_map/ppermute | solution.py:187
  17.5 10.6 %collective-permute-start.7 = (f32[40,128]{1,0:T(8,128)S(1)}, f32[40,128]{1,0:T(8,128)S(1)}, u32[]{:S(2)}, u32[]{:S(2)}) collective-permute-start(f32[40,128]{1,0:T(8,128)S(1)} %shard_map.53.b0), channel_id=1, source_target_pairs={{0,2},{1,3},{2,0},{3,1},{4,6},{5,7},{6,4},{7,5},{8,10},{9,11},{10,... | collective-permute-start | bytes 61448 | tf_op jit(solution)/shard_map/ppermute | solution.py:187
  20.2 7.9 %collective-permute-start.6 = (f32[40,128]{1,0:T(8,128)S(1)}, f32[40,128]{1,0:T(8,128)S(1)}, u32[]{:S(2)}, u32[]{:S(2)}) collective-permute-start(f32[40,128]{1,0:T(8,128)S(1)} %shard_map.53.b0), channel_id=1, source_target_pairs={{0,3},{1,0},{2,1},{3,2},{4,7},{5,4},{6,5},{7,6},{8,11},{9,8},{10,9... | collective-permute-start | bytes 61448 | tf_op jit(solution)/shard_map/ppermute | solution.py:187
  29.0 17.6 %all-to-all-start.1 = ((f32[64,4,128]{2,1,0:T(4,128)}), f32[64,4,128]{2,1,0:T(4,128)S(1)}, u32[]{:S(2)}, u32[]{:S(2)}) async-start(f32[64,4,128]{2,1,0:T(4,128)} %shard_map.54), calls=%async_computation.1 | async-start | bytes 262144 | tf_op jit(solution)/shard_map/all_to_all | solution.py:210
  35.3 8.0 %collective-permute-start = (f32[208,128]{1,0:T(8,128)S(1)}, f32[208,128]{1,0:T(8,128)S(1)}, u32[]{:S(2)}, u32[]{:S(2)}) collective-permute-start(f32[208,128]{1,0:T(8,128)S(1)} %get-tuple-element.12.y2), channel_id=1, source_target_pairs={{0,2},{1,3},{2,0},{3,1},{4,6},{5,7},{6,4},{7,5},{8,10},{9,11},{10,... | collective-permute-start | bytes 319496 | tf_op jit(solution)/shard_map/ppermute | solution.py:187
  38.4 7.0 %collective-permute-start.1 = (f32[208,128]{1,0:T(8,128)S(1)}, f32[208,128]{1,0:T(8,128)S(1)}, u32[]{:S(2)}, u32[]{:S(2)}) collective-permute-start(f32[208,128]{1,0:T(8,128)S(1)} %get-tuple-element.13.y1), channel_id=1, source_target_pairs={{0,1},{1,2},{2,3},{3,0},{4,5},{5,6},{6,7},{7,4},{8,9},{9,10},{10,1... | collective-permute-start | bytes 319496 | tf_op jit(solution)/shard_map/ppermute | solution.py:187
  39.0 6.5 %collective-permute-start.2 = (f32[208,128]{1,0:T(8,128)S(1)}, f32[208,128]{1,0:T(8,128)S(1)}, u32[]{:S(2)}, u32[]{:S(2)}) collective-permute-start(f32[208,128]{1,0:T(8,128)S(1)} %get-tuple-element.14.y3), channel_id=1, source_target_pairs={{0,3},{1,0},{2,1},{3,2},{4,7},{5,4},{6,5},{7,6},{8,11},{9,8},{10,9... | collective-permute-start | bytes 319496 | tf_op jit(solution)/shard_map/ppermute | solution.py:187

commit v3 on v2

--- a/solution.py
+++ b/solution.py
@@ -120,7 +120,11 @@
     pay_ref[...] = jnp.broadcast_to(jnp.concatenate(pay, axis=1)[None], pay_ref.shape)
 
 
-def finish_kernel(y0, y1, y2, y3, x_ref, y_ref, out_ref, held_ref, sem):
+def add_kernel(x_ref, out_ref):
+    out_ref[...] = jnp.sum(x_ref[...].reshape(8, 4, 4, 128), axis=0)
+
+
+def finish_kernel(y0, y1, y2, y3, x0, x1, y_ref, out_ref, held_ref, sem):
     def total(at):
         return (y0[at, :] + y1[at, :]) + (y2[at, :] + y3[at, :])
 
@@ -134,7 +138,7 @@
     copy = pltpu.make_async_copy(held_ref, y_ref, sem)
     copy.start()
     gram_k = unfold(total(slice(BODY, MSG)))
-    x = jnp.sum(x_ref[...].reshape(16, 4, 4, 128), axis=0)
+    x = x0[...] + x1[...]
     d = jnp.concatenate([x[q][:, 96 : 96 + R] for q in range(4)], axis=0)
     x = (x[0] + x[1]) + (x[2] + x[3])
     lane, sub = lanes_of((4, 16)), sublanes_of((4, 16))
@@ -193,25 +197,27 @@
     factor_k = pltpu.with_memory_space_constraint(factor_k, pltpu.HBM)
     tensor = pltpu.with_memory_space_constraint(tensor, pltpu.HBM)
     j0 = factor_j.T
-    js = [shift(j0, "ia", s, 4) for s in (1, 2, 3)]
+    js = {s: shift(j0, "ia", s, 4) for s in (1, 3, 2)}
     k_own, j_own = call(
         own_kernel, [sds((R, 64), bf16), sds((16, R), bf16)], [HB, HB], 0, 0, [dma((2,))]
     )(factor_k, pltpu.with_memory_space_constraint(j0, pltpu.HBM))
     packed = call(pack_kernel, sds((16, 16, 128), bf16), [VM])(k_own)
     c = lax.all_to_all(packed, ("z", "c"), 0, 0, tiled=True)
-    b = call(factor_kernel, sds((40, 128), f32), [VM] * 4, 2**33, 2**20)(j_own, *js)
-    bs = [b] + [shift(b, "ka", 4 - s, 4) for s in (1, 2, 3)]
+    b = call(factor_kernel, sds((40, 128), f32), [VM] * 4, 2**33, 2**20)(j_own, js[1], js[2], js[3])
+    bs = {s: shift(b, "ka", 4 - s, 4) for s in (1, 3, 2)}
     msgs = call(
         contract_kernel, [sds((MSG, 128), f32)] * 4, [VM, HB], 2**34, 2**23,
         [pltpu.VMEM((4, 16, 64, 1024), bf16), dma((4,))],
     )(c, tensor)
     got = {s: shift(msgs[s], "ka", s, 4) for s in (2, 1, 3)}
-    pay = call(partial_kernel, sds((64, 4, 128), f32), [VM] * 8)(*msgs, *bs)
-    pay = lax.all_to_all(pay, ("z", "c", "ka"), 0, 0, tiled=True)
+    pay = call(partial_kernel, sds((32, 4, 128), f32), [VM] * 8)(*msgs, b, bs[1], bs[2], bs[3])
+    pay = lax.all_to_all(pay, ("z", "ka"), 0, 0, tiled=True)
+    pay = call(add_kernel, sds((4, 4, 128), f32), [VM])(pay)
+    other = lax.ppermute(pay, "c", [(0, 1), (1, 0)])
     y, new_factor = call(
-        finish_kernel, [sds((400, 64), f32), sds((16, R), f32)], [VM] * 5, 0, 0,
+        finish_kernel, [sds((400, 64), f32), sds((16, R), f32)], [VM] * 6, 0, 0,
         [pltpu.VMEM((400, 64), f32), dma(())], [HB, VM],
-    )(msgs[0], got[2], got[1], got[3], pay)
+    )(msgs[0], got[2], got[1], got[3], pay, other)
     return y.reshape(R, 16, 64), new_factor.T
 
 

time: 49 us -> 49.1 us (level)
  the two profiles are of different devices: /device:TPU:8 before, /device:TPU:1 now
where the time goes in v3:
time: 49.1 us; the launch traced here: 48.7 us
  starting transfers between devices  32.1 us (65%)
  Pallas kernels  9.14 us (19%)
  waiting for transfers between devices  6.81 us (14%)
  between operations  0.71 us (1%)
    ppermute x9, starting transfers between devices, shift(): return lax.ppermute(x, axis, [(i, (i + by) % n) for i in range(n)])  15.1 us
    all_to_all x1, starting transfers between devices, per_device(): c = lax.all_to_all(packed, ('z', 'c'), 0, 0, tiled=True)  9.99 us
    all_to_all x1, starting transfers between devices, per_device(): pay = lax.all_to_all(pay, ('z', 'ka'), 0, 0, tiled=True)  4.7 us
    pallas_call x1, Pallas kernels, per_device(): call(contract_kernel, [sds((MSG, 128), f32)] * 4, [VM, HB], 2 ** 34, 2 **...  4.53 us
    all_to_all x1, waiting for transfers between devices, per_device(): pay = lax.all_to_all(pay, ('z', 'ka'), 0, 0, tiled=True)  3.33 us
    all_to_all x1, waiting for transfers between devices, per_device(): c = lax.all_to_all(packed, ('z', 'c'), 0, 0, tiled=True)  2.64 us
    ppermute x1, starting transfers between devices, per_device(): other = lax.ppermute(pay, 'c', [(0, 1), (1, 0)])  2.33 us
    pallas_call x1, Pallas kernels, per_device(): call(finish_kernel, [sds((400, 64), f32), sds((16, R), f32)], [VM] * 6, 0...  2.04 us
  transfers between devices with their start and end apart: 12, of which 3 were waited for; matrix products, arithmetic and copies ran while one was open for 0% of the time, Pallas kernels for 13%

profile of v3, /device:TPU:1, one launch (start us, length us, event | category | flops | bytes accessed | tf_op | source)
XLA Modules:
  0.0 48.7 jit_solution(7258446918985056300)
XLA Ops:
  0.6 3.6 %collective-permute-start.5 = (bf16[16,25]{1,0:T(8,128)(2,1)}, bf16[16,25]{1,0:T(8,128)(2,1)S(1)}, u32[]{:S(2)}, u32[]{:S(2)}) collective-permute-start(bf16[16,25]{1,0:T(8,128)(2,1)} %bitcast.3), channel_id=1, source_target_pairs={{0,192},{64,0},{128,64},{192,128},{1,193},{65,1},{129,65},{193,129... | collective-permute-start | bytes 2408 | tf_op jit(solution)/shard_map/ppermute | solution.py:191
  4.3 0.3 collective-permute-start.4
  4.6 0.7 %collective-permute-start.3 = (bf16[16,25]{1,0:T(8,128)(2,1)}, bf16[16,25]{1,0:T(8,128)(2,1)S(1)}, u32[]{:S(2)}, u32[]{:S(2)}) collective-permute-start(bf16[16,25]{1,0:T(8,128)(2,1)} %bitcast.5), channel_id=1, source_target_pairs={{0,64},{64,128},{128,192},{192,0},{1,65},{65,129},{129,193},{193,1... | collective-permute-start | bytes 2408 | tf_op jit(solution)/shard_map/ppermute | solution.py:191
  5.3 0.7 %shard_map.50 = (bf16[25,64]{1,0:T(8,128)(2,1)S(1)}, bf16[16,25]{1,0:T(8,128)(2,1)S(1)}) custom-call(bf16[25,64]{1,0:T(8,128)(2,1)} %k_ref.1, bf16[16,25]{1,0:T(8,128)(2,1)} %bitcast.6), custom_call_target="tpu_custom_call" | custom-call | tf_op jit(solution)/shard_map/pallas_call | solution.py:201
  6.1 0.7 %shard_map.51 = bf16[16,16,128]{2,1,0:T(8,128)(2,1)} custom-call(bf16[25,64]{1,0:T(8,128)(2,1)S(1)} %get-tuple-element.10.k_ref), custom_call_target="tpu_custom_call" | custom-call | tf_op jit(solution)/shard_map/pallas_call | solution.py:204
  6.8 10.0 %all-to-all-start = ((bf16[16,16,128]{2,1,0:T(8,128)(2,1)}), bf16[16,16,128]{2,1,0:T(8,128)(2,1)S(1)}, u32[]{:S(2)}, u32[]{:S(2)}) async-start(bf16[16,16,128]{2,1,0:T(8,128)(2,1)} %shard_map.51), calls=%async_computation | async-start | bytes 131072 | tf_op jit(solution)/shard_map/all_to_all | solution.py:205
  16.8 0.0 collective-permute-done.5.j3
  16.8 0.0 collective-permute-done.4.j2
  16.8 0.0 collective-permute-done.3.j1
  16.8 0.3 shard_map.53.b0
  17.0 1.3 %collective-permute-start.8 = (f32[40,128]{1,0:T(8,128)S(1)}, f32[40,128]{1,0:T(8,128)S(1)}, u32[]{:S(2)}, u32[]{:S(2)}) collective-permute-start(f32[40,128]{1,0:T(8,128)S(1)} %shard_map.53.b0), channel_id=1, source_target_pairs={{0,1},{1,2},{2,3},{3,0},{4,5},{5,6},{6,7},{7,4},{8,9},{9,10},{10,1... | collective-permute-start | bytes 61448 | tf_op jit(solution)/shard_map/ppermute | solution.py:191
  18.3 2.5 %collective-permute-start.7 = (f32[40,128]{1,0:T(8,128)S(1)}, f32[40,128]{1,0:T(8,128)S(1)}, u32[]{:S(2)}, u32[]{:S(2)}) collective-permute-start(f32[40,128]{1,0:T(8,128)S(1)} %shard_map.53.b0), channel_id=1, source_target_pairs={{0,2},{1,3},{2,0},{3,1},{4,6},{5,7},{6,4},{7,5},{8,10},{9,11},{10,... | collective-permute-start | bytes 61448 | tf_op jit(solution)/shard_map/ppermute | solution.py:191
  20.8 1.2 %collective-permute-start.6 = (f32[40,128]{1,0:T(8,128)S(1)}, f32[40,128]{1,0:T(8,128)S(1)}, u32[]{:S(2)}, u32[]{:S(2)}) collective-permute-start(f32[40,128]{1,0:T(8,128)S(1)} %shard_map.53.b0), channel_id=1, source_target_pairs={{0,3},{1,0},{2,1},{3,2},{4,7},{5,4},{6,5},{7,6},{8,11},{9,8},{10,9... | collective-permute-start | bytes 61448 | tf_op jit(solution)/shard_map/ppermute | solution.py:191
  21.9 2.6 %all-to-all-done.c_ref = bf16[16,16,128]{2,1,0:T(8,128)(2,1)S(1)} async-done(((bf16[16,16,128]{2,1,0:T(8,128)(2,1)}), bf16[16,16,128]{2,1,0:T(8,128)(2,1)S(1)}, u32[]{:S(2)}, u32[]{:S(2)}) %all-to-all-start) | async-done | bytes 65568 | tf_op jit(solution)/shard_map/all_to_all | solution.py:205
  24.6 4.5 %shard_map.52 = (f32[208,128]{1,0:T(8,128)S(1)}, f32[208,128]{1,0:T(8,128)S(1)}, f32[208,128]{1,0:T(8,128)S(1)}, f32[208,128]{1,0:T(8,128)S(1)}) custom-call(bf16[16,16,128]{2,1,0:T(8,128)(2,1)S(1)} %all-to-all-done.c_ref, bf16[16,256,1024]{2,1,0:T(8,128)(2,1)} %t_ref.1), custom_call_target="tpu_custom_call" | custom-call | flops 17179869184 | bytes 8388608 | tf_op jit(solution)/shard_map/pallas_call | solution.py:208
  29.1 0.0 collective-permute-done.8.b3
  29.1 0.0 collective-permute-done.7.b2
  29.1 0.0 collective-permute-done.6.b1
  29.1 0.9 %shard_map.54 = f32[32,4,128]{2,1,0:T(4,128)} custom-call(f32[208,128]{1,0:T(8,128)S(1)} %get-tuple-element.11.y0, f32[208,128]{1,0:T(8,128)S(1)} %get-tuple-element.13.y1, f32[208,128]{1,0:T(8,128)S(1)} %get-tuple-element.12.y2, f32[208,128]{1,0:T(8,128)S(1)} %get-tuple-element.14.y3, f32[40,128]{1,0:T(8,128)S(1)} %shard_map.53.b0, ...), custom_call_target="tpu_custom_call" | custom-call | tf_op jit(solution)/shard_map/pallas_call | solution.py:213
  30.0 4.7 %all-to-all-start.1 = ((f32[32,4,128]{2,1,0:T(4,128)}), f32[32,4,128]{2,1,0:T(4,128)S(1)}, u32[]{:S(2)}, u32[]{:S(2)}) async-start(f32[32,4,128]{2,1,0:T(4,128)} %shard_map.54), calls=%async_computation.1 | async-start | bytes 131072 | tf_op jit(solution)/shard_map/all_to_all | solution.py:214
  34.7 2.8 %collective-permute-start = (f32[208,128]{1,0:T(8,128)S(1)}, f32[208,128]{1,0:T(8,128)S(1)}, u32[]{:S(2)}, u32[]{:S(2)}) collective-permute-start(f32[208,128]{1,0:T(8,128)S(1)} %get-tuple-element.12.y2), channel_id=1, source_target_pairs={{0,2},{1,3},{2,0},{3,1},{4,6},{5,7},{6,4},{7,5},{8,10},{9,11},{10,... | collective-permute-start | bytes 319496 | tf_op jit(solution)/shard_map/ppermute | solution.py:191
  37.5 0.3 collective-permute-start.1
  37.8 2.4 %collective-permute-start.2 = (f32[208,128]{1,0:T(8,128)S(1)}, f32[208,128]{1,0:T(8,128)S(1)}, u32[]{:S(2)}, u32[]{:S(2)}) collective-permute-start(f32[208,128]{1,0:T(8,128)S(1)} %get-tuple-element.14.y3), channel_id=1, source_target_pairs={{0,3},{1,0},{2,1},{3,2},{4,7},{5,4},{6,5},{7,6},{8,11},{9,8},{10,9... | collective-permute-start | bytes 319496 | tf_op jit(solution)/shard_map/ppermute | solution.py:191
  40.2 3.3 %all-to-all-done.1.x_ref = f32[32,4,128]{2,1,0:T(4,128)S(1)} async-done(((f32[32,4,128]{2,1,0:T(4,128)}), f32[32,4,128]{2,1,0:T(4,128)S(1)}, u32[]{:S(2)}, u32[]{:S(2)}) %all-to-all-start.1) | async-done | bytes 65568 | tf_op jit(solution)/shard_map/all_to_all | solution.py:214
  43.6 2.3 %collective-permute-start.9 = (f32[4,4,128]{2,1,0:T(4,128)S(1)}, f32[4,4,128]{2,1,0:T(4,128)S(1)}, u32[]{:S(2)}, u32[]{:S(2)}) collective-permute-start(f32[4,4,128]{2,1,0:T(4,128)S(1)} %shard_map.55.x0), channel_id=1, source_target_pairs={{0,4},{4,0},{1,5},{5,1},{2,6},{6,2},{3,7},{7,3},{8,12},{12,8},{9,1... | collective-permute-start | bytes 24584 | tf_op jit(solution)/shard_map/ppermute | solution.py:216
  45.9 0.0 collective-permute-done.y1
  45.9 0.0 collective-permute-done.1.y2
  45.9 0.0 collective-permute-done.2.y3
  45.9 0.8 %collective-permute-done.9.x1 = f32[4,4,128]{2,1,0:T(4,128)S(1)} collective-permute-done((f32[4,4,128]{2,1,0:T(4,128)S(1)}, f32[4,4,128]{2,1,0:T(4,128)S(1)}, u32[]{:S(2)}, u32[]{:S(2)}) %collective-permute-start.9) | collective-permute-done | bytes 8224 | tf_op jit(solution)/shard_map/ppermute | solution.py:216
  46.7 2.0 %shard_map.56 = (f32[400,64]{1,0:T(8,128)}, f32[16,25]{1,0:T(8,128)}) custom-call(f32[208,128]{1,0:T(8,128)S(1)} %get-tuple-element.11.y0, f32[208,128]{1,0:T(8,128)S(1)} %collective-permute-done.y1, f32[208,128]{1,0:T(8,128)S(1)} %collective-permute-done.1.y2, f32[208,128]{1,0:T(8,128)S(1)} %collective-permute-done.2.y3, f32[4,4,128]{2,1,0:T(4,128)S(1)} %shard_map.55.x0, ...), custom_call_target="tpu_custom_call" | custom-call | tf_op jit(solution)/shard_map/pallas_call | solution.py:217
  (1 shorter events, 0.0 us)
Async XLA Ops:
  0.6 16.1 %collective-permute-start.5 = (bf16[16,25]{1,0:T(8,128)(2,1)}, bf16[16,25]{1,0:T(8,128)(2,1)S(1)}, u32[]{:S(2)}, u32[]{:S(2)}) collective-permute-start(bf16[16,25]{1,0:T(8,128)(2,1)} %bitcast.3), channel_id=1, source_target_pairs={{0,192},{64,0},{128,64},{192,128},{1,193},{65,1},{129,65},{193,129... | collective-permute-start | bytes 2408 | tf_op jit(solution)/shard_map/ppermute | solution.py:191
  4.3 12.5 %collective-permute-start.4 = (bf16[16,25]{1,0:T(8,128)(2,1)}, bf16[16,25]{1,0:T(8,128)(2,1)S(1)}, u32[]{:S(2)}, u32[]{:S(2)}) collective-permute-start(bf16[16,25]{1,0:T(8,128)(2,1)} %bitcast.4), channel_id=1, source_target_pairs={{0,128},{64,192},{128,0},{192,64},{1,129},{65,193},{129,1},{193,65... | collective-permute-start | bytes 2408 | tf_op jit(solution)/shard_map/ppermute | solution.py:191
  4.6 12.2 %collective-permute-start.3 = (bf16[16,25]{1,0:T(8,128)(2,1)}, bf16[16,25]{1,0:T(8,128)(2,1)S(1)}, u32[]{:S(2)}, u32[]{:S(2)}) collective-permute-start(bf16[16,25]{1,0:T(8,128)(2,1)} %bitcast.5), channel_id=1, source_target_pairs={{0,64},{64,128},{128,192},{192,0},{1,65},{65,129},{129,193},{193,1... | collective-permute-start | bytes 2408 | tf_op jit(solution)/shard_map/ppermute | solution.py:191
  6.8 17.8 %all-to-all-start = ((bf16[16,16,128]{2,1,0:T(8,128)(2,1)}), bf16[16,16,128]{2,1,0:T(8,128)(2,1)S(1)}, u32[]{:S(2)}, u32[]{:S(2)}) async-start(bf16[16,16,128]{2,1,0:T(8,128)(2,1)} %shard_map.51), calls=%async_computation | async-start | bytes 131072 | tf_op jit(solution)/shard_map/all_to_all | solution.py:205
  17.0 12.1 %collective-permute-start.8 = (f32[40,128]{1,0:T(8,128)S(1)}, f32[40,128]{1,0:T(8,128)S(1)}, u32[]{:S(2)}, u32[]{:S(2)}) collective-permute-start(f32[40,128]{1,0:T(8,128)S(1)} %shard_map.53.b0), channel_id=1, source_target_pairs={{0,1},{1,2},{2,3},{3,0},{4,5},{5,6},{6,7},{7,4},{8,9},{9,10},{10,1... | collective-permute-start | bytes 61448 | tf_op jit(solution)/shard_map/ppermute | solution.py:191
  18.3 10.8 %collective-permute-start.7 = (f32[40,128]{1,0:T(8,128)S(1)}, f32[40,128]{1,0:T(8,128)S(1)}, u32[]{:S(2)}, u32[]{:S(2)}) collective-permute-start(f32[40,128]{1,0:T(8,128)S(1)} %shard_map.53.b0), channel_id=1, source_target_pairs={{0,2},{1,3},{2,0},{3,1},{4,6},{5,7},{6,4},{7,5},{8,10},{9,11},{10,... | collective-permute-start | bytes 61448 | tf_op jit(solution)/shard_map/ppermute | solution.py:191
  20.8 8.4 %collective-permute-start.6 = (f32[40,128]{1,0:T(8,128)S(1)}, f32[40,128]{1,0:T(8,128)S(1)}, u32[]{:S(2)}, u32[]{:S(2)}) collective-permute-start(f32[40,128]{1,0:T(8,128)S(1)} %shard_map.53.b0), channel_id=1, source_target_pairs={{0,3},{1,0},{2,1},{3,2},{4,7},{5,4},{6,5},{7,6},{8,11},{9,8},{10,9... | collective-permute-start | bytes 61448 | tf_op jit(solution)/shard_map/ppermute | solution.py:191
  30.0 13.5 %all-to-all-start.1 = ((f32[32,4,128]{2,1,0:T(4,128)}), f32[32,4,128]{2,1,0:T(4,128)S(1)}, u32[]{:S(2)}, u32[]{:S(2)}) async-start(f32[32,4,128]{2,1,0:T(4,128)} %shard_map.54), calls=%async_computation.1 | async-start | bytes 131072 | tf_op jit(solution)/shard_map/all_to_all | solution.py:214
  34.7 11.2 %collective-permute-start = (f32[208,128]{1,0:T(8,128)S(1)}, f32[208,128]{1,0:T(8,128)S(1)}, u32[]{:S(2)}, u32[]{:S(2)}) collective-permute-start(f32[208,128]{1,0:T(8,128)S(1)} %get-tuple-element.12.y2), channel_id=1, source_target_pairs={{0,2},{1,3},{2,0},{3,1},{4,6},{5,7},{6,4},{7,5},{8,10},{9,11},{10,... | collective-permute-start | bytes 319496 | tf_op jit(solution)/shard_map/ppermute | solution.py:191
  37.5 8.4 %collective-permute-start.1 = (f32[208,128]{1,0:T(8,128)S(1)}, f32[208,128]{1,0:T(8,128)S(1)}, u32[]{:S(2)}, u32[]{:S(2)}) collective-permute-start(f32[208,128]{1,0:T(8,128)S(1)} %get-tuple-element.13.y1), channel_id=1, source_target_pairs={{0,1},{1,2},{2,3},{3,0},{4,5},{5,6},{6,7},{7,4},{8,9},{9,10},{10,1... | collective-permute-start | bytes 319496 | tf_op jit(solution)/shard_map/ppermute | solution.py:191
  37.8 8.1 %collective-permute-start.2 = (f32[208,128]{1,0:T(8,128)S(1)}, f32[208,128]{1,0:T(8,128)S(1)}, u32[]{:S(2)}, u32[]{:S(2)}) collective-permute-start(f32[208,128]{1,0:T(8,128)S(1)} %get-tuple-element.14.y3), channel_id=1, source_target_pairs={{0,3},{1,0},{2,1},{3,2},{4,7},{5,4},{6,5},{7,6},{8,11},{9,8},{10,9... | collective-permute-start | bytes 319496 | tf_op jit(solution)/shard_map/ppermute | solution.py:191
  43.6 3.2 %collective-permute-start.9 = (f32[4,4,128]{2,1,0:T(4,128)S(1)}, f32[4,4,128]{2,1,0:T(4,128)S(1)}, u32[]{:S(2)}, u32[]{:S(2)}) collective-permute-start(f32[4,4,128]{2,1,0:T(4,128)S(1)} %shard_map.55.x0), channel_id=1, source_target_pairs={{0,4},{4,0},{1,5},{5,1},{2,6},{6,2},{3,7},{7,3},{8,12},{12,8},{9,1... | collective-permute-start | bytes 24584 | tf_op jit(solution)/shard_map/ppermute | solution.py:216

commit v4 on v3

--- a/solution.py
+++ b/solution.py
@@ -124,20 +124,22 @@
     out_ref[...] = jnp.sum(x_ref[...].reshape(8, 4, 4, 128), axis=0)
 
 
-def finish_kernel(y0, y1, y2, y3, x0, x1, y_ref, out_ref, held_ref, sem):
+def sum_kernel(y0, y1, y2, y3, y_ref, gk_ref):
     def total(at):
         return (y0[at, :] + y1[at, :]) + (y2[at, :] + y3[at, :])
 
     for t in range(TILES):
         s = total(slice(24 * t, 24 * t + 24))
-        held_ref[pl.ds(2 * t, 24, stride=16), :] = s[:, 0:64]
-        held_ref[pl.ds(2 * t + 1, 24, stride=16), :] = s[:, 64:128]
+        y_ref[pl.ds(2 * t, 24, stride=16), :] = s[:, 0:64]
+        y_ref[pl.ds(2 * t + 1, 24, stride=16), :] = s[:, 64:128]
     s = total(slice(192, 200))
-    held_ref[pl.ds(384, 8, stride=2), :] = s[:, 0:64]
-    held_ref[pl.ds(385, 8, stride=2), :] = s[:, 64:128]
-    copy = pltpu.make_async_copy(held_ref, y_ref, sem)
-    copy.start()
-    gram_k = unfold(total(slice(BODY, MSG)))
+    y_ref[pl.ds(384, 8, stride=2), :] = s[:, 0:64]
+    y_ref[pl.ds(385, 8, stride=2), :] = s[:, 64:128]
+    gk_ref[...] = total(slice(BODY, MSG))
+
+
+def solve_kernel(x0, x1, gk_ref, out_ref):
+    gram_k = unfold(gk_ref[...])
     x = x0[...] + x1[...]
     d = jnp.concatenate([x[q][:, 96 : 96 + R] for q in range(4)], axis=0)
     x = (x[0] + x[1]) + (x[2] + x[3])
@@ -172,7 +174,6 @@
             a = eliminate(a)
             cols[q + 1 :] = [eliminate(x) for x in cols[q + 1 :]]
     out_ref[...] = pad_rows(a, 128).T[32:48, 0:R]
-    copy.wait()
 
 
 def call(kernel, out, specs, flops=0, nbytes=0, scratch=(), out_specs=None):
@@ -214,10 +215,10 @@
     pay = lax.all_to_all(pay, ("z", "ka"), 0, 0, tiled=True)
     pay = call(add_kernel, sds((4, 4, 128), f32), [VM])(pay)
     other = lax.ppermute(pay, "c", [(0, 1), (1, 0)])
-    y, new_factor = call(
-        finish_kernel, [sds((400, 64), f32), sds((16, R), f32)], [VM] * 6, 0, 0,
-        [pltpu.VMEM((400, 64), f32), dma(())], [HB, VM],
-    )(msgs[0], got[2], got[1], got[3], pay, other)
+    y, gram_k = call(sum_kernel, [sds((400, 64), f32), sds((8, 128), f32)], [VM] * 4, 0, 2**21)(
+        msgs[0], got[2], got[1], got[3]
+    )
+    new_factor = call(solve_kernel, sds((16, R), f32), [VM] * 3)(pay, other, gram_k)
     return y.reshape(R, 16, 64), new_factor.T
 
 

time: 49.1 us -> 48.4 us (0.986)
  waiting for transfers between devices: 6.81 us -> 6 us
    ppermute x1, waiting for transfers between devices: 0.82 us -> 0.01 us  [per_device(): other = lax.ppermute(pay, 'c', [(0, 1), (1, 0)])]
    pallas_call x1 -> x2, Pallas kernels: 2.04 us -> 2.19 us  [the longest x1 1.39 us: per_device(): call(solve_kernel, sds((16, R), f32), [VM] * 3)(pay, other, gram_k)]
  transfers between devices with their start and end apart: 12 -> 12, of which waited for: 3 -> 2; matrix products, arithmetic and copies ran while one was open for 0% -> 0% of each run, Pallas kernels for 13% -> 15%
where the time goes in v4:
time: 48.4 us; the launch traced here: 48.1 us
  starting transfers between devices  32.1 us (66%)
  Pallas kernels  9.3 us (19%)
  waiting for transfers between devices  6 us (12%)
  between operations  0.71 us (1%)
    ppermute x9, starting transfers between devices, shift(): return lax.ppermute(x, axis, [(i, (i + by) % n) for i in range(n)])  15.1 us
    all_to_all x1, starting transfers between devices, per_device(): c = lax.all_to_all(packed, ('z', 'c'), 0, 0, tiled=True)  9.99 us
    all_to_all x1, starting transfers between devices, per_device(): pay = lax.all_to_all(pay, ('z', 'ka'), 0, 0, tiled=True)  4.7 us
    pallas_call x1, Pallas kernels, per_device(): call(contract_kernel, [sds((MSG, 128), f32)] * 4, [VM, HB], 2 ** 34, 2 **...  4.53 us
    all_to_all x1, waiting for transfers between devices, per_device(): pay = lax.all_to_all(pay, ('z', 'ka'), 0, 0, tiled=True)  3.33 us
    all_to_all x1, waiting for transfers between devices, per_device(): c = lax.all_to_all(packed, ('z', 'c'), 0, 0, tiled=True)  2.64 us
    ppermute x1, starting transfers between devices, per_device(): other = lax.ppermute(pay, 'c', [(0, 1), (1, 0)])  2.33 us
    pallas_call x1, Pallas kernels, per_device(): call(solve_kernel, sds((16, R), f32), [VM] * 3)(pay, other, gram_k)  1.39 us
  transfers between devices with their start and end apart: 12, of which 2 were waited for; matrix products, arithmetic and copies ran while one was open for 0% of the time, Pallas kernels for 15%

profile of v4, /device:TPU:1, one launch (start us, length us, event | category | flops | bytes accessed | tf_op | source)
XLA Modules:
  0.0 48.1 jit_solution(13907445085932704152)
XLA Ops:
  0.6 3.6 %collective-permute-start.5 = (bf16[16,25]{1,0:T(8,128)(2,1)}, bf16[16,25]{1,0:T(8,128)(2,1)S(1)}, u32[]{:S(2)}, u32[]{:S(2)}) collective-permute-start(bf16[16,25]{1,0:T(8,128)(2,1)} %bitcast.4), channel_id=1, source_target_pairs={{0,192},{64,0},{128,64},{192,128},{1,193},{65,1},{129,65},{193,129... | collective-permute-start | bytes 2408 | tf_op jit(solution)/shard_map/ppermute | solution.py:192
  4.3 0.3 collective-permute-start.4
  4.6 0.7 %collective-permute-start.3 = (bf16[16,25]{1,0:T(8,128)(2,1)}, bf16[16,25]{1,0:T(8,128)(2,1)S(1)}, u32[]{:S(2)}, u32[]{:S(2)}) collective-permute-start(bf16[16,25]{1,0:T(8,128)(2,1)} %bitcast.6), channel_id=1, source_target_pairs={{0,64},{64,128},{128,192},{192,0},{1,65},{65,129},{129,193},{193,1... | collective-permute-start | bytes 2408 | tf_op jit(solution)/shard_map/ppermute | solution.py:192
  5.3 0.7 %shard_map.50 = (bf16[25,64]{1,0:T(8,128)(2,1)S(1)}, bf16[16,25]{1,0:T(8,128)(2,1)S(1)}) custom-call(bf16[25,64]{1,0:T(8,128)(2,1)} %k_ref.1, bf16[16,25]{1,0:T(8,128)(2,1)} %bitcast.7), custom_call_target="tpu_custom_call" | custom-call | tf_op jit(solution)/shard_map/pallas_call | solution.py:202
  6.1 0.7 %shard_map.51 = bf16[16,16,128]{2,1,0:T(8,128)(2,1)} custom-call(bf16[25,64]{1,0:T(8,128)(2,1)S(1)} %get-tuple-element.10.k_ref), custom_call_target="tpu_custom_call" | custom-call | tf_op jit(solution)/shard_map/pallas_call | solution.py:205
  6.8 10.0 %all-to-all-start = ((bf16[16,16,128]{2,1,0:T(8,128)(2,1)}), bf16[16,16,128]{2,1,0:T(8,128)(2,1)S(1)}, u32[]{:S(2)}, u32[]{:S(2)}) async-start(bf16[16,16,128]{2,1,0:T(8,128)(2,1)} %shard_map.51), calls=%async_computation | async-start | bytes 131072 | tf_op jit(solution)/shard_map/all_to_all | solution.py:206
  16.8 0.0 collective-permute-done.5.j3
  16.8 0.0 collective-permute-done.4.j2
  16.8 0.0 collective-permute-done.3.j1
  16.8 0.3 shard_map.54.b0
  17.0 1.3 %collective-permute-start.8 = (f32[40,128]{1,0:T(8,128)S(1)}, f32[40,128]{1,0:T(8,128)S(1)}, u32[]{:S(2)}, u32[]{:S(2)}) collective-permute-start(f32[40,128]{1,0:T(8,128)S(1)} %shard_map.54.b0), channel_id=1, source_target_pairs={{0,1},{1,2},{2,3},{3,0},{4,5},{5,6},{6,7},{7,4},{8,9},{9,10},{10,1... | collective-permute-start | bytes 61448 | tf_op jit(solution)/shard_map/ppermute | solution.py:192
  18.3 2.5 %collective-permute-start.7 = (f32[40,128]{1,0:T(8,128)S(1)}, f32[40,128]{1,0:T(8,128)S(1)}, u32[]{:S(2)}, u32[]{:S(2)}) collective-permute-start(f32[40,128]{1,0:T(8,128)S(1)} %shard_map.54.b0), channel_id=1, source_target_pairs={{0,2},{1,3},{2,0},{3,1},{4,6},{5,7},{6,4},{7,5},{8,10},{9,11},{10,... | collective-permute-start | bytes 61448 | tf_op jit(solution)/shard_map/ppermute | solution.py:192
  20.8 1.2 %collective-permute-start.6 = (f32[40,128]{1,0:T(8,128)S(1)}, f32[40,128]{1,0:T(8,128)S(1)}, u32[]{:S(2)}, u32[]{:S(2)}) collective-permute-start(f32[40,128]{1,0:T(8,128)S(1)} %shard_map.54.b0), channel_id=1, source_target_pairs={{0,3},{1,0},{2,1},{3,2},{4,7},{5,4},{6,5},{7,6},{8,11},{9,8},{10,9... | collective-permute-start | bytes 61448 | tf_op jit(solution)/shard_map/ppermute | solution.py:192
  21.9 2.6 %all-to-all-done.c_ref = bf16[16,16,128]{2,1,0:T(8,128)(2,1)S(1)} async-done(((bf16[16,16,128]{2,1,0:T(8,128)(2,1)}), bf16[16,16,128]{2,1,0:T(8,128)(2,1)S(1)}, u32[]{:S(2)}, u32[]{:S(2)}) %all-to-all-start) | async-done | bytes 65568 | tf_op jit(solution)/shard_map/all_to_all | solution.py:206
  24.6 4.5 %shard_map.52 = (f32[208,128]{1,0:T(8,128)S(1)}, f32[208,128]{1,0:T(8,128)S(1)}, f32[208,128]{1,0:T(8,128)S(1)}, f32[208,128]{1,0:T(8,128)S(1)}) custom-call(bf16[16,16,128]{2,1,0:T(8,128)(2,1)S(1)} %all-to-all-done.c_ref, bf16[16,256,1024]{2,1,0:T(8,128)(2,1)} %t_ref.1), custom_call_target="tpu_custom_call" | custom-call | flops 17179869184 | bytes 8388608 | tf_op jit(solution)/shard_map/pallas_call | solution.py:209
  29.1 0.0 collective-permute-done.8.b3
  29.1 0.0 collective-permute-done.7.b2
  29.1 0.0 collective-permute-done.6.b1
  29.1 0.9 %shard_map.55 = f32[32,4,128]{2,1,0:T(4,128)} custom-call(f32[208,128]{1,0:T(8,128)S(1)} %get-tuple-element.11.y0, f32[208,128]{1,0:T(8,128)S(1)} %get-tuple-element.13.y1, f32[208,128]{1,0:T(8,128)S(1)} %get-tuple-element.12.y2, f32[208,128]{1,0:T(8,128)S(1)} %get-tuple-element.14.y3, f32[40,128]{1,0:T(8,128)S(1)} %shard_map.54.b0, ...), custom_call_target="tpu_custom_call" | custom-call | tf_op jit(solution)/shard_map/pallas_call | solution.py:214
  30.0 4.7 %all-to-all-start.1 = ((f32[32,4,128]{2,1,0:T(4,128)}), f32[32,4,128]{2,1,0:T(4,128)S(1)}, u32[]{:S(2)}, u32[]{:S(2)}) async-start(f32[32,4,128]{2,1,0:T(4,128)} %shard_map.55), calls=%async_computation.1 | async-start | bytes 131072 | tf_op jit(solution)/shard_map/all_to_all | solution.py:215
  34.7 2.8 %collective-permute-start = (f32[208,128]{1,0:T(8,128)S(1)}, f32[208,128]{1,0:T(8,128)S(1)}, u32[]{:S(2)}, u32[]{:S(2)}) collective-permute-start(f32[208,128]{1,0:T(8,128)S(1)} %get-tuple-element.12.y2), channel_id=1, source_target_pairs={{0,2},{1,3},{2,0},{3,1},{4,6},{5,7},{6,4},{7,5},{8,10},{9,11},{10,... | collective-permute-start | bytes 319496 | tf_op jit(solution)/shard_map/ppermute | solution.py:192
  37.5 0.3 collective-permute-start.1
  37.8 2.4 %collective-permute-start.2 = (f32[208,128]{1,0:T(8,128)S(1)}, f32[208,128]{1,0:T(8,128)S(1)}, u32[]{:S(2)}, u32[]{:S(2)}) collective-permute-start(f32[208,128]{1,0:T(8,128)S(1)} %get-tuple-element.14.y3), channel_id=1, source_target_pairs={{0,3},{1,0},{2,1},{3,2},{4,7},{5,4},{6,5},{7,6},{8,11},{9,8},{10,9... | collective-permute-start | bytes 319496 | tf_op jit(solution)/shard_map/ppermute | solution.py:192
  40.2 3.3 %all-to-all-done.1.x_ref = f32[32,4,128]{2,1,0:T(4,128)S(1)} async-done(((f32[32,4,128]{2,1,0:T(4,128)}), f32[32,4,128]{2,1,0:T(4,128)S(1)}, u32[]{:S(2)}, u32[]{:S(2)}) %all-to-all-start.1) | async-done | bytes 65568 | tf_op jit(solution)/shard_map/all_to_all | solution.py:215
  43.6 2.3 %collective-permute-start.9 = (f32[4,4,128]{2,1,0:T(4,128)S(1)}, f32[4,4,128]{2,1,0:T(4,128)S(1)}, u32[]{:S(2)}, u32[]{:S(2)}) collective-permute-start(f32[4,4,128]{2,1,0:T(4,128)S(1)} %shard_map.56.x0), channel_id=1, source_target_pairs={{0,4},{4,0},{1,5},{5,1},{2,6},{6,2},{3,7},{7,3},{8,12},{12,8},{9,1... | collective-permute-start | bytes 24584 | tf_op jit(solution)/shard_map/ppermute | solution.py:217
  45.9 0.0 collective-permute-done.y1
  45.9 0.0 collective-permute-done.1.y2
  45.9 0.0 collective-permute-done.2.y3
  45.9 0.8 %shard_map.53 = (f32[400,64]{1,0:T(8,128)}, f32[8,128]{1,0:T(8,128)S(1)}) custom-call(f32[208,128]{1,0:T(8,128)S(1)} %get-tuple-element.11.y0, f32[208,128]{1,0:T(8,128)S(1)} %collective-permute-done.y1, f32[208,128]{1,0:T(8,128)S(1)} %collective-permute-done.1.y2, f32[208,128]{1,0:T(8,128)S(1)} %collective-permute-done.2.y3), custom_call_target="tpu_custom_call" | custom-call | bytes 2097152 | tf_op jit(solution)/shard_map/pallas_call | solution.py:218
  46.7 0.0 collective-permute-done.9.x1
  46.7 1.4 %shard_map.57 = f32[16,25]{1,0:T(8,128)} custom-call(f32[4,4,128]{2,1,0:T(4,128)S(1)} %shard_map.56.x0, f32[4,4,128]{2,1,0:T(4,128)S(1)} %collective-permute-done.9.x1, f32[8,128]{1,0:T(8,128)S(1)} %get-tuple-element.17.gk_ref), custom_call_target="tpu_custom_call" | custom-call | tf_op jit(solution)/shard_map/pallas_call | solution.py:221
  (1 shorter events, 0.0 us)
Async XLA Ops:
  0.6 16.1 %collective-permute-start.5 = (bf16[16,25]{1,0:T(8,128)(2,1)}, bf16[16,25]{1,0:T(8,128)(2,1)S(1)}, u32[]{:S(2)}, u32[]{:S(2)}) collective-permute-start(bf16[16,25]{1,0:T(8,128)(2,1)} %bitcast.4), channel_id=1, source_target_pairs={{0,192},{64,0},{128,64},{192,128},{1,193},{65,1},{129,65},{193,129... | collective-permute-start | bytes 2408 | tf_op jit(solution)/shard_map/ppermute | solution.py:192
  4.3 12.5 %collective-permute-start.4 = (bf16[16,25]{1,0:T(8,128)(2,1)}, bf16[16,25]{1,0:T(8,128)(2,1)S(1)}, u32[]{:S(2)}, u32[]{:S(2)}) collective-permute-start(bf16[16,25]{1,0:T(8,128)(2,1)} %bitcast.5), channel_id=1, source_target_pairs={{0,128},{64,192},{128,0},{192,64},{1,129},{65,193},{129,1},{193,65... | collective-permute-start | bytes 2408 | tf_op jit(solution)/shard_map/ppermute | solution.py:192
  4.6 12.2 %collective-permute-start.3 = (bf16[16,25]{1,0:T(8,128)(2,1)}, bf16[16,25]{1,0:T(8,128)(2,1)S(1)}, u32[]{:S(2)}, u32[]{:S(2)}) collective-permute-start(bf16[16,25]{1,0:T(8,128)(2,1)} %bitcast.6), channel_id=1, source_target_pairs={{0,64},{64,128},{128,192},{192,0},{1,65},{65,129},{129,193},{193,1... | collective-permute-start | bytes 2408 | tf_op jit(solution)/shard_map/ppermute | solution.py:192
  6.8 17.8 %all-to-all-start = ((bf16[16,16,128]{2,1,0:T(8,128)(2,1)}), bf16[16,16,128]{2,1,0:T(8,128)(2,1)S(1)}, u32[]{:S(2)}, u32[]{:S(2)}) async-start(bf16[16,16,128]{2,1,0:T(8,128)(2,1)} %shard_map.51), calls=%async_computation | async-start | bytes 131072 | tf_op jit(solution)/shard_map/all_to_all | solution.py:206
  17.0 12.1 %collective-permute-start.8 = (f32[40,128]{1,0:T(8,128)S(1)}, f32[40,128]{1,0:T(8,128)S(1)}, u32[]{:S(2)}, u32[]{:S(2)}) collective-permute-start(f32[40,128]{1,0:T(8,128)S(1)} %shard_map.54.b0), channel_id=1, source_target_pairs={{0,1},{1,2},{2,3},{3,0},{4,5},{5,6},{6,7},{7,4},{8,9},{9,10},{10,1... | collective-permute-start | bytes 61448 | tf_op jit(solution)/shard_map/ppermute | solution.py:192
  18.3 10.8 %collective-permute-start.7 = (f32[40,128]{1,0:T(8,128)S(1)}, f32[40,128]{1,0:T(8,128)S(1)}, u32[]{:S(2)}, u32[]{:S(2)}) collective-permute-start(f32[40,128]{1,0:T(8,128)S(1)} %shard_map.54.b0), channel_id=1, source_target_pairs={{0,2},{1,3},{2,0},{3,1},{4,6},{5,7},{6,4},{7,5},{8,10},{9,11},{10,... | collective-permute-start | bytes 61448 | tf_op jit(solution)/shard_map/ppermute | solution.py:192
  20.8 8.4 %collective-permute-start.6 = (f32[40,128]{1,0:T(8,128)S(1)}, f32[40,128]{1,0:T(8,128)S(1)}, u32[]{:S(2)}, u32[]{:S(2)}) collective-permute-start(f32[40,128]{1,0:T(8,128)S(1)} %shard_map.54.b0), channel_id=1, source_target_pairs={{0,3},{1,0},{2,1},{3,2},{4,7},{5,4},{6,5},{7,6},{8,11},{9,8},{10,9... | collective-permute-start | bytes 61448 | tf_op jit(solution)/shard_map/ppermute | solution.py:192
  30.0 13.5 %all-to-all-start.1 = ((f32[32,4,128]{2,1,0:T(4,128)}), f32[32,4,128]{2,1,0:T(4,128)S(1)}, u32[]{:S(2)}, u32[]{:S(2)}) async-start(f32[32,4,128]{2,1,0:T(4,128)} %shard_map.55), calls=%async_computation.1 | async-start | bytes 131072 | tf_op jit(solution)/shard_map/all_to_all | solution.py:215
  34.7 11.2 %collective-permute-start = (f32[208,128]{1,0:T(8,128)S(1)}, f32[208,128]{1,0:T(8,128)S(1)}, u32[]{:S(2)}, u32[]{:S(2)}) collective-permute-start(f32[208,128]{1,0:T(8,128)S(1)} %get-tuple-element.12.y2), channel_id=1, source_target_pairs={{0,2},{1,3},{2,0},{3,1},{4,6},{5,7},{6,4},{7,5},{8,10},{9,11},{10,... | collective-permute-start | bytes 319496 | tf_op jit(solution)/shard_map/ppermute | solution.py:192
  37.5 8.4 %collective-permute-start.1 = (f32[208,128]{1,0:T(8,128)S(1)}, f32[208,128]{1,0:T(8,128)S(1)}, u32[]{:S(2)}, u32[]{:S(2)}) collective-permute-start(f32[208,128]{1,0:T(8,128)S(1)} %get-tuple-element.13.y1), channel_id=1, source_target_pairs={{0,1},{1,2},{2,3},{3,0},{4,5},{5,6},{6,7},{7,4},{8,9},{9,10},{10,1... | collective-permute-start | bytes 319496 | tf_op jit(solution)/shard_map/ppermute | solution.py:192
  37.8 8.1 %collective-permute-start.2 = (f32[208,128]{1,0:T(8,128)S(1)}, f32[208,128]{1,0:T(8,128)S(1)}, u32[]{:S(2)}, u32[]{:S(2)}) collective-permute-start(f32[208,128]{1,0:T(8,128)S(1)} %get-tuple-element.14.y3), channel_id=1, source_target_pairs={{0,3},{1,0},{2,1},{3,2},{4,7},{5,4},{6,5},{7,6},{8,11},{9,8},{10,9... | collective-permute-start | bytes 319496 | tf_op jit(solution)/shard_map/ppermute | solution.py:192
  43.6 3.2 %collective-permute-start.9 = (f32[4,4,128]{2,1,0:T(4,128)S(1)}, f32[4,4,128]{2,1,0:T(4,128)S(1)}, u32[]{:S(2)}, u32[]{:S(2)}) collective-permute-start(f32[4,4,128]{2,1,0:T(4,128)S(1)} %shard_map.56.x0), channel_id=1, source_target_pairs={{0,4},{4,0},{1,5},{5,1},{2,6},{6,2},{3,7},{7,3},{8,12},{12,8},{9,1... | collective-permute-start | bytes 24584 | tf_op jit(solution)/shard_map/ppermute | solution.py:217

commit v5 on v4

--- a/solution.py
+++ b/solution.py
@@ -39,7 +39,7 @@
 def transposed(x):
     rows = -(-x.shape[1] // 8) * 8
     x = jnp.concatenate([x, jnp.zeros((x.shape[0], 128 - x.shape[1]), x.dtype)], axis=1)
-    return pad_rows(x, 128).T[0:rows, 0 : x.shape[0]]
+    return x.T[0:rows]
 
 
 def own_kernel(k_ref, j_ref, kout_ref, jout_ref, sems):
@@ -173,7 +173,7 @@
 
             a = eliminate(a)
             cols[q + 1 :] = [eliminate(x) for x in cols[q + 1 :]]
-    out_ref[...] = pad_rows(a, 128).T[32:48, 0:R]
+    out_ref[...] = a.T[32:48, 0:R]
 
 
 def call(kernel, out, specs, flops=0, nbytes=0, scratch=(), out_specs=None):

time: 48.4 us -> 48.4 us (level)
  no operation moved by 1% of the time
where the time goes in v5:
time: 48.4 us; the launch traced here: 48.1 us
  starting transfers between devices  32.1 us (66%)
  Pallas kernels  9.3 us (19%)
  waiting for transfers between devices  6 us (12%)
  between operations  0.71 us (1%)
    ppermute x9, starting transfers between devices, shift(): return lax.ppermute(x, axis, [(i, (i + by) % n) for i in range(n)])  15.1 us
    all_to_all x1, starting transfers between devices, per_device(): c = lax.all_to_all(packed, ('z', 'c'), 0, 0, tiled=True)  9.99 us
    all_to_all x1, starting transfers between devices, per_device(): pay = lax.all_to_all(pay, ('z', 'ka'), 0, 0, tiled=True)  4.7 us
    pallas_call x1, Pallas kernels, per_device(): call(contract_kernel, [sds((MSG, 128), f32)] * 4, [VM, HB], 2 ** 34, 2 **...  4.53 us
    all_to_all x1, waiting for transfers between devices, per_device(): pay = lax.all_to_all(pay, ('z', 'ka'), 0, 0, tiled=True)  3.33 us
    all_to_all x1, waiting for transfers between devices, per_device(): c = lax.all_to_all(packed, ('z', 'c'), 0, 0, tiled=True)  2.64 us
    ppermute x1, starting transfers between devices, per_device(): other = lax.ppermute(pay, 'c', [(0, 1), (1, 0)])  2.33 us
    pallas_call x1, Pallas kernels, per_device(): call(solve_kernel, sds((16, R), f32), [VM] * 3)(pay, other, gram_k)  1.39 us
  transfers between devices with their start and end apart: 12, of which 2 were waited for; matrix products, arithmetic and copies ran while one was open for 0% of the time, Pallas kernels for 15%

profile of v5, /device:TPU:1, one launch (start us, length us, event | category | flops | bytes accessed | tf_op | source)
XLA Modules:
  0.0 48.1 jit_solution(13907445085932704152)
XLA Ops:
  0.6 3.6 %collective-permute-start.5 = (bf16[16,25]{1,0:T(8,128)(2,1)}, bf16[16,25]{1,0:T(8,128)(2,1)S(1)}, u32[]{:S(2)}, u32[]{:S(2)}) collective-permute-start(bf16[16,25]{1,0:T(8,128)(2,1)} %bitcast.4), channel_id=1, source_target_pairs={{0,192},{64,0},{128,64},{192,128},{1,193},{65,1},{129,65},{193,129... | collective-permute-start | bytes 2408 | tf_op jit(solution)/shard_map/ppermute | solution.py:192
  4.3 0.3 collective-permute-start.4
  4.6 0.7 %collective-permute-start.3 = (bf16[16,25]{1,0:T(8,128)(2,1)}, bf16[16,25]{1,0:T(8,128)(2,1)S(1)}, u32[]{:S(2)}, u32[]{:S(2)}) collective-permute-start(bf16[16,25]{1,0:T(8,128)(2,1)} %bitcast.6), channel_id=1, source_target_pairs={{0,64},{64,128},{128,192},{192,0},{1,65},{65,129},{129,193},{193,1... | collective-permute-start | bytes 2408 | tf_op jit(solution)/shard_map/ppermute | solution.py:192
  5.3 0.7 %shard_map.50 = (bf16[25,64]{1,0:T(8,128)(2,1)S(1)}, bf16[16,25]{1,0:T(8,128)(2,1)S(1)}) custom-call(bf16[25,64]{1,0:T(8,128)(2,1)} %k_ref.1, bf16[16,25]{1,0:T(8,128)(2,1)} %bitcast.7), custom_call_target="tpu_custom_call" | custom-call | tf_op jit(solution)/shard_map/pallas_call | solution.py:202
  6.1 0.7 %shard_map.51 = bf16[16,16,128]{2,1,0:T(8,128)(2,1)} custom-call(bf16[25,64]{1,0:T(8,128)(2,1)S(1)} %get-tuple-element.10.k_ref), custom_call_target="tpu_custom_call" | custom-call | tf_op jit(solution)/shard_map/pallas_call | solution.py:205
  6.8 10.0 %all-to-all-start = ((bf16[16,16,128]{2,1,0:T(8,128)(2,1)}), bf16[16,16,128]{2,1,0:T(8,128)(2,1)S(1)}, u32[]{:S(2)}, u32[]{:S(2)}) async-start(bf16[16,16,128]{2,1,0:T(8,128)(2,1)} %shard_map.51), calls=%async_computation | async-start | bytes 131072 | tf_op jit(solution)/shard_map/all_to_all | solution.py:206
  16.8 0.0 collective-permute-done.5.j3
  16.8 0.0 collective-permute-done.4.j2
  16.8 0.0 collective-permute-done.3.j1
  16.8 0.3 shard_map.54.b0
  17.0 1.3 %collective-permute-start.8 = (f32[40,128]{1,0:T(8,128)S(1)}, f32[40,128]{1,0:T(8,128)S(1)}, u32[]{:S(2)}, u32[]{:S(2)}) collective-permute-start(f32[40,128]{1,0:T(8,128)S(1)} %shard_map.54.b0), channel_id=1, source_target_pairs={{0,1},{1,2},{2,3},{3,0},{4,5},{5,6},{6,7},{7,4},{8,9},{9,10},{10,1... | collective-permute-start | bytes 61448 | tf_op jit(solution)/shard_map/ppermute | solution.py:192
  18.3 2.5 %collective-permute-start.7 = (f32[40,128]{1,0:T(8,128)S(1)}, f32[40,128]{1,0:T(8,128)S(1)}, u32[]{:S(2)}, u32[]{:S(2)}) collective-permute-start(f32[40,128]{1,0:T(8,128)S(1)} %shard_map.54.b0), channel_id=1, source_target_pairs={{0,2},{1,3},{2,0},{3,1},{4,6},{5,7},{6,4},{7,5},{8,10},{9,11},{10,... | collective-permute-start | bytes 61448 | tf_op jit(solution)/shard_map/ppermute | solution.py:192
  20.8 1.2 %collective-permute-start.6 = (f32[40,128]{1,0:T(8,128)S(1)}, f32[40,128]{1,0:T(8,128)S(1)}, u32[]{:S(2)}, u32[]{:S(2)}) collective-permute-start(f32[40,128]{1,0:T(8,128)S(1)} %shard_map.54.b0), channel_id=1, source_target_pairs={{0,3},{1,0},{2,1},{3,2},{4,7},{5,4},{6,5},{7,6},{8,11},{9,8},{10,9... | collective-permute-start | bytes 61448 | tf_op jit(solution)/shard_map/ppermute | solution.py:192
  21.9 2.6 %all-to-all-done.c_ref = bf16[16,16,128]{2,1,0:T(8,128)(2,1)S(1)} async-done(((bf16[16,16,128]{2,1,0:T(8,128)(2,1)}), bf16[16,16,128]{2,1,0:T(8,128)(2,1)S(1)}, u32[]{:S(2)}, u32[]{:S(2)}) %all-to-all-start) | async-done | bytes 65568 | tf_op jit(solution)/shard_map/all_to_all | solution.py:206
  24.6 4.5 %shard_map.52 = (f32[208,128]{1,0:T(8,128)S(1)}, f32[208,128]{1,0:T(8,128)S(1)}, f32[208,128]{1,0:T(8,128)S(1)}, f32[208,128]{1,0:T(8,128)S(1)}) custom-call(bf16[16,16,128]{2,1,0:T(8,128)(2,1)S(1)} %all-to-all-done.c_ref, bf16[16,256,1024]{2,1,0:T(8,128)(2,1)} %t_ref.1), custom_call_target="tpu_custom_call" | custom-call | flops 17179869184 | bytes 8388608 | tf_op jit(solution)/shard_map/pallas_call | solution.py:209
  29.1 0.0 collective-permute-done.8.b3
  29.1 0.0 collective-permute-done.7.b2
  29.1 0.0 collective-permute-done.6.b1
  29.1 0.9 %shard_map.55 = f32[32,4,128]{2,1,0:T(4,128)} custom-call(f32[208,128]{1,0:T(8,128)S(1)} %get-tuple-element.11.y0, f32[208,128]{1,0:T(8,128)S(1)} %get-tuple-element.13.y1, f32[208,128]{1,0:T(8,128)S(1)} %get-tuple-element.12.y2, f32[208,128]{1,0:T(8,128)S(1)} %get-tuple-element.14.y3, f32[40,128]{1,0:T(8,128)S(1)} %shard_map.54.b0, ...), custom_call_target="tpu_custom_call" | custom-call | tf_op jit(solution)/shard_map/pallas_call | solution.py:214
  30.0 4.7 %all-to-all-start.1 = ((f32[32,4,128]{2,1,0:T(4,128)}), f32[32,4,128]{2,1,0:T(4,128)S(1)}, u32[]{:S(2)}, u32[]{:S(2)}) async-start(f32[32,4,128]{2,1,0:T(4,128)} %shard_map.55), calls=%async_computation.1 | async-start | bytes 131072 | tf_op jit(solution)/shard_map/all_to_all | solution.py:215
  34.7 2.8 %collective-permute-start = (f32[208,128]{1,0:T(8,128)S(1)}, f32[208,128]{1,0:T(8,128)S(1)}, u32[]{:S(2)}, u32[]{:S(2)}) collective-permute-start(f32[208,128]{1,0:T(8,128)S(1)} %get-tuple-element.12.y2), channel_id=1, source_target_pairs={{0,2},{1,3},{2,0},{3,1},{4,6},{5,7},{6,4},{7,5},{8,10},{9,11},{10,... | collective-permute-start | bytes 319496 | tf_op jit(solution)/shard_map/ppermute | solution.py:192
  37.5 0.3 collective-permute-start.1
  37.8 2.4 %collective-permute-start.2 = (f32[208,128]{1,0:T(8,128)S(1)}, f32[208,128]{1,0:T(8,128)S(1)}, u32[]{:S(2)}, u32[]{:S(2)}) collective-permute-start(f32[208,128]{1,0:T(8,128)S(1)} %get-tuple-element.14.y3), channel_id=1, source_target_pairs={{0,3},{1,0},{2,1},{3,2},{4,7},{5,4},{6,5},{7,6},{8,11},{9,8},{10,9... | collective-permute-start | bytes 319496 | tf_op jit(solution)/shard_map/ppermute | solution.py:192
  40.2 3.3 %all-to-all-done.1.x_ref = f32[32,4,128]{2,1,0:T(4,128)S(1)} async-done(((f32[32,4,128]{2,1,0:T(4,128)}), f32[32,4,128]{2,1,0:T(4,128)S(1)}, u32[]{:S(2)}, u32[]{:S(2)}) %all-to-all-start.1) | async-done | bytes 65568 | tf_op jit(solution)/shard_map/all_to_all | solution.py:215
  43.6 2.3 %collective-permute-start.9 = (f32[4,4,128]{2,1,0:T(4,128)S(1)}, f32[4,4,128]{2,1,0:T(4,128)S(1)}, u32[]{:S(2)}, u32[]{:S(2)}) collective-permute-start(f32[4,4,128]{2,1,0:T(4,128)S(1)} %shard_map.56.x0), channel_id=1, source_target_pairs={{0,4},{4,0},{1,5},{5,1},{2,6},{6,2},{3,7},{7,3},{8,12},{12,8},{9,1... | collective-permute-start | bytes 24584 | tf_op jit(solution)/shard_map/ppermute | solution.py:217
  45.9 0.0 collective-permute-done.y1
  45.9 0.0 collective-permute-done.1.y2
  45.9 0.0 collective-permute-done.2.y3
  45.9 0.8 %shard_map.53 = (f32[400,64]{1,0:T(8,128)}, f32[8,128]{1,0:T(8,128)S(1)}) custom-call(f32[208,128]{1,0:T(8,128)S(1)} %get-tuple-element.11.y0, f32[208,128]{1,0:T(8,128)S(1)} %collective-permute-done.y1, f32[208,128]{1,0:T(8,128)S(1)} %collective-permute-done.1.y2, f32[208,128]{1,0:T(8,128)S(1)} %collective-permute-done.2.y3), custom_call_target="tpu_custom_call" | custom-call | bytes 2097152 | tf_op jit(solution)/shard_map/pallas_call | solution.py:218
  46.7 0.0 collective-permute-done.9.x1
  46.7 1.4 %shard_map.57 = f32[16,25]{1,0:T(8,128)} custom-call(f32[4,4,128]{2,1,0:T(4,128)S(1)} %shard_map.56.x0, f32[4,4,128]{2,1,0:T(4,128)S(1)} %collective-permute-done.9.x1, f32[8,128]{1,0:T(8,128)S(1)} %get-tuple-element.17.gk_ref), custom_call_target="tpu_custom_call" | custom-call | tf_op jit(solution)/shard_map/pallas_call | solution.py:221
  (1 shorter events, 0.0 us)
Async XLA Ops:
  0.6 16.1 %collective-permute-start.5 = (bf16[16,25]{1,0:T(8,128)(2,1)}, bf16[16,25]{1,0:T(8,128)(2,1)S(1)}, u32[]{:S(2)}, u32[]{:S(2)}) collective-permute-start(bf16[16,25]{1,0:T(8,128)(2,1)} %bitcast.4), channel_id=1, source_target_pairs={{0,192},{64,0},{128,64},{192,128},{1,193},{65,1},{129,65},{193,129... | collective-permute-start | bytes 2408 | tf_op jit(solution)/shard_map/ppermute | solution.py:192
  4.3 12.5 %collective-permute-start.4 = (bf16[16,25]{1,0:T(8,128)(2,1)}, bf16[16,25]{1,0:T(8,128)(2,1)S(1)}, u32[]{:S(2)}, u32[]{:S(2)}) collective-permute-start(bf16[16,25]{1,0:T(8,128)(2,1)} %bitcast.5), channel_id=1, source_target_pairs={{0,128},{64,192},{128,0},{192,64},{1,129},{65,193},{129,1},{193,65... | collective-permute-start | bytes 2408 | tf_op jit(solution)/shard_map/ppermute | solution.py:192
  4.6 12.2 %collective-permute-start.3 = (bf16[16,25]{1,0:T(8,128)(2,1)}, bf16[16,25]{1,0:T(8,128)(2,1)S(1)}, u32[]{:S(2)}, u32[]{:S(2)}) collective-permute-start(bf16[16,25]{1,0:T(8,128)(2,1)} %bitcast.6), channel_id=1, source_target_pairs={{0,64},{64,128},{128,192},{192,0},{1,65},{65,129},{129,193},{193,1... | collective-permute-start | bytes 2408 | tf_op jit(solution)/shard_map/ppermute | solution.py:192
  6.8 17.8 %all-to-all-start = ((bf16[16,16,128]{2,1,0:T(8,128)(2,1)}), bf16[16,16,128]{2,1,0:T(8,128)(2,1)S(1)}, u32[]{:S(2)}, u32[]{:S(2)}) async-start(bf16[16,16,128]{2,1,0:T(8,128)(2,1)} %shard_map.51), calls=%async_computation | async-start | bytes 131072 | tf_op jit(solution)/shard_map/all_to_all | solution.py:206
  17.0 12.1 %collective-permute-start.8 = (f32[40,128]{1,0:T(8,128)S(1)}, f32[40,128]{1,0:T(8,128)S(1)}, u32[]{:S(2)}, u32[]{:S(2)}) collective-permute-start(f32[40,128]{1,0:T(8,128)S(1)} %shard_map.54.b0), channel_id=1, source_target_pairs={{0,1},{1,2},{2,3},{3,0},{4,5},{5,6},{6,7},{7,4},{8,9},{9,10},{10,1... | collective-permute-start | bytes 61448 | tf_op jit(solution)/shard_map/ppermute | solution.py:192
  18.3 10.8 %collective-permute-start.7 = (f32[40,128]{1,0:T(8,128)S(1)}, f32[40,128]{1,0:T(8,128)S(1)}, u32[]{:S(2)}, u32[]{:S(2)}) collective-permute-start(f32[40,128]{1,0:T(8,128)S(1)} %shard_map.54.b0), channel_id=1, source_target_pairs={{0,2},{1,3},{2,0},{3,1},{4,6},{5,7},{6,4},{7,5},{8,10},{9,11},{10,... | collective-permute-start | bytes 61448 | tf_op jit(solution)/shard_map/ppermute | solution.py:192
  20.8 8.4 %collective-permute-start.6 = (f32[40,128]{1,0:T(8,128)S(1)}, f32[40,128]{1,0:T(8,128)S(1)}, u32[]{:S(2)}, u32[]{:S(2)}) collective-permute-start(f32[40,128]{1,0:T(8,128)S(1)} %shard_map.54.b0), channel_id=1, source_target_pairs={{0,3},{1,0},{2,1},{3,2},{4,7},{5,4},{6,5},{7,6},{8,11},{9,8},{10,9... | collective-permute-start | bytes 61448 | tf_op jit(solution)/shard_map/ppermute | solution.py:192
  30.0 13.5 %all-to-all-start.1 = ((f32[32,4,128]{2,1,0:T(4,128)}), f32[32,4,128]{2,1,0:T(4,128)S(1)}, u32[]{:S(2)}, u32[]{:S(2)}) async-start(f32[32,4,128]{2,1,0:T(4,128)} %shard_map.55), calls=%async_computation.1 | async-start | bytes 131072 | tf_op jit(solution)/shard_map/all_to_all | solution.py:215
  34.7 11.2 %collective-permute-start = (f32[208,128]{1,0:T(8,128)S(1)}, f32[208,128]{1,0:T(8,128)S(1)}, u32[]{:S(2)}, u32[]{:S(2)}) collective-permute-start(f32[208,128]{1,0:T(8,128)S(1)} %get-tuple-element.12.y2), channel_id=1, source_target_pairs={{0,2},{1,3},{2,0},{3,1},{4,6},{5,7},{6,4},{7,5},{8,10},{9,11},{10,... | collective-permute-start | bytes 319496 | tf_op jit(solution)/shard_map/ppermute | solution.py:192
  37.5 8.4 %collective-permute-start.1 = (f32[208,128]{1,0:T(8,128)S(1)}, f32[208,128]{1,0:T(8,128)S(1)}, u32[]{:S(2)}, u32[]{:S(2)}) collective-permute-start(f32[208,128]{1,0:T(8,128)S(1)} %get-tuple-element.13.y1), channel_id=1, source_target_pairs={{0,1},{1,2},{2,3},{3,0},{4,5},{5,6},{6,7},{7,4},{8,9},{9,10},{10,1... | collective-permute-start | bytes 319496 | tf_op jit(solution)/shard_map/ppermute | solution.py:192
  37.8 8.1 %collective-permute-start.2 = (f32[208,128]{1,0:T(8,128)S(1)}, f32[208,128]{1,0:T(8,128)S(1)}, u32[]{:S(2)}, u32[]{:S(2)}) collective-permute-start(f32[208,128]{1,0:T(8,128)S(1)} %get-tuple-element.14.y3), channel_id=1, source_target_pairs={{0,3},{1,0},{2,1},{3,2},{4,7},{5,4},{6,5},{7,6},{8,11},{9,8},{10,9... | collective-permute-start | bytes 319496 | tf_op jit(solution)/shard_map/ppermute | solution.py:192
  43.6 3.2 %collective-permute-start.9 = (f32[4,4,128]{2,1,0:T(4,128)S(1)}, f32[4,4,128]{2,1,0:T(4,128)S(1)}, u32[]{:S(2)}, u32[]{:S(2)}) collective-permute-start(f32[4,4,128]{2,1,0:T(4,128)S(1)} %shard_map.56.x0), channel_id=1, source_target_pairs={{0,4},{4,0},{1,5},{5,1},{2,6},{6,2},{3,7},{7,3},{8,12},{12,8},{9,1... | collective-permute-start | bytes 24584 | tf_op jit(solution)/shard_map/ppermute | solution.py:217
